TPU v7x, 32 devices: a whole 2x2x4 slice. The times are simulated.
32 devices in a mesh: sens: 8 (over y, x, core), hour: 4 (over z).
Axes of the slice: x: 2, y: 2, z: 4, core: 2. Of those that a mesh axis runs over, the one named last changes fastest.
Arguments:
- sky: bfloat16 [512, 146], P('hour'), may hold values from 0.049804688 to 1
- sky_open: bfloat16 [146, 16384], P(None, 'sens'), may hold values from 0 to 0.013977051
- sky_closed: bfloat16 [146, 16384], P(None, 'sens'), may hold values from 0 to 0.0039978027
- sun_coef: bfloat16 [5165, 16384], P(None, ('sens', 'hour')), may hold values from 0 to 1
- sun_bins: int32 [512, 4], P('hour'), may hold values from 0 to 5164, as said below
- sun_rad: bfloat16 [512, 4], P('hour'), may hold values from 0.099609375 to 1
- target: bfloat16 [512, 16384], P('hour', 'sens'), may hold values from 0 to 2
- zone_of: int32 [8192, 1], P('sens'), may hold values from 0 to 7
- area: float32 [8192], P('sens'), may hold values from 0.5 to 4
- openness: float32 [8192], P('sens'), may hold values from 0 to 1
Outputs:
- illuminance: bfloat16 [512, 16384], P('hour', 'sens')
- new_openness: float32 [8192], P('sens')
Inputs may be any that keep to these rules, and one draw needn't show every extreme that they name: `sun_bins`: the 4 bins of one hour are consecutive modulo 5165, hence distinct. `zone_of`: every zone has at least one window.
All inputs are finite; a program needn't handle non-finite values.
Results may differ from a plain program's by a relative error of at most 0.001.
Values may be sent and summed in bfloat16 or wider, within the bound.
No kernel may reach another device: no remote copies, remote signals or barrier semaphores. Data moves between devices by JAX's collectives and lax.ppermute only.
A program may use at most 128 MiB of HBM per device.

v0:
```python
import jax
import jax.numpy as jnp
from jax import lax
from jax.experimental import pallas as pl
from jax.experimental.pallas import tpu as pltpu
from jax.sharding import PartitionSpec as P

LANES = 128
CHUNK = 8
HEAD = 16
TAIL = 8
PATTERN = jnp.bfloat16
LEVELS = 65000.0
VMEM_BYTES = 12 * 1024 * 1024
ANY = pl.BlockSpec(memory_space=pl.ANY)
HBM = pl.BlockSpec(memory_space=pltpu.HBM)
SMEM = pl.BlockSpec(memory_space=pltpu.SMEM)
VMEM = pl.BlockSpec(memory_space=pltpu.VMEM)


def call(kernel, name, out_shape, flops=0, moved=0, **more):
    run = pl.pallas_call(
        kernel,
        out_shape=out_shape,
        name=name,
        compiler_params=pltpu.CompilerParams(vmem_limit_bytes=VMEM_BYTES),
        cost_estimate=pl.CostEstimate(flops=flops, bytes_accessed=moved, transcendentals=0),
        **more,
    )
    specs = more["in_specs"]
    return lambda *args: run(
        *[pltpu.with_memory_space_constraint(x, pltpu.HBM) if s is HBM else x for x, s in zip(args, specs)]
    )


def exchange(x, axis, mask):
    return lax.ppermute(x, axis, [(i, i ^ mask) for i in range(lax.axis_size(axis))])


def fetch(pairs, sems):
    copies = [pltpu.make_async_copy(source, place, sems.at[i]) for i, (source, place) in enumerate(pairs)]
    for c in copies:
        c.start()
    return copies


def pack_kernel(bins_hbm, rad_hbm, out_ref, bins_ref, rad_ref, sems):
    for c in fetch([(bins_hbm, bins_ref), (rad_hbm, rad_ref)], sems):
        c.wait()
    bins = bins_ref[:]
    kbins = bins.shape[0]
    fill = jnp.zeros((HEAD - 3 * kbins, bins.shape[1]), jnp.float32)
    parts = [rad_ref[:].astype(jnp.float32), (bins // LANES).astype(jnp.float32), (bins % LANES).astype(jnp.float32)]
    out_ref[:] = jnp.concatenate(parts + [fill], axis=0).astype(jnp.bfloat16)


def fetch_kernel(zones):
    def kernel(coef_hbm, zone_hbm, area_hbm, openness_hbm, coef_ref, sums_ref, zone_ref, area_ref, openness_ref, sems):
        pairs = [(zone_hbm, zone_ref), (area_hbm, area_ref), (openness_hbm, openness_ref)]
        copies = fetch(pairs + [(coef_hbm.at[pl.ds(0, coef_ref.shape[0])], coef_ref)], sems)
        for c in copies[:3]:
            c.wait()
        zone, area = zone_ref[:], area_ref[:]
        lane = lax.broadcasted_iota(jnp.int32, sums_ref.shape, 1)
        values = [area * openness_ref[:], area, area * area]
        row = jnp.zeros(sums_ref.shape, jnp.float32)
        for z in range(zones):
            member = zone == z
            for k, value in enumerate(values):
                total = jnp.sum(jnp.where(member, value, 0.0), keepdims=True)
                row = jnp.where(lane == (2 + k) * zones + z, total, row)
        sums_ref[:] = row
        copies[3].wait()

    return kernel


def sun_kernel(count, kbins, stream):
    def kernel(first_ref, rest_in, *refs):
        heads, outs, rest = refs[:count], refs[count : 2 * count], refs[2 * count :]
        rows = heads[0].shape[1]
        split = first_ref.shape[0]
        nbins = split + rest_in.shape[0] - (split if stream else 0)
        step = CHUNK * LANES
        spans = [(first, min(first + step, nbins)) for first in range(0, nbins, step)]
        if stream:
            rest_ref, acc, pattern, block, sems = rest
            late = [span for span in spans if span[0] >= split]
            cuts = late[:-2] + [(late[-2][0], nbins)]
            copies = fetch(
                [
                    (rest_in.at[pl.ds(first, end - first)], rest_ref.at[pl.ds(first - split, end - first)])
                    for first, end in cuts
                ],
                sems,
            )
            waits = {first: c for (first, _), c in zip(cuts, copies)}
        else:
            rest_ref, (acc, pattern, block) = rest_in, rest
            waits = {}
        lane = lax.broadcasted_iota(jnp.int32, (rows, LANES), 1)
        for g in range(count):
            small = heads[g][:].astype(jnp.float32).T
            value = jnp.zeros((rows, LANES), jnp.float32)
            where = jnp.zeros((rows, LANES), jnp.float32)
            for k in range(kbins):
                low = small[:, 2 * kbins + k : 2 * kbins + k + 1].astype(jnp.int32)
                hit = lane == low
                value = jnp.where(hit, small[:, k : k + 1], value)
                where = jnp.where(hit, small[:, kbins + k : kbins + k + 1], where)
            pattern[g * rows : (g + 1) * rows] = value.astype(pattern.dtype)
            block[g * rows : (g + 1) * rows] = where.astype(block.dtype)

        for first, end in spans:
            parts = []
            for c in range(first // LANES, pl.cdiv(end, LANES)):
                here = block[:] == jnp.asarray(c, block.dtype)
                parts.append(jnp.where(here, pattern[:], jnp.zeros_like(pattern)).astype(jnp.bfloat16))
            weights = jnp.concatenate(parts, axis=1) if len(parts) > 1 else parts[0]
            if first in waits:
                waits[first].wait()
            coef = first_ref[first:end] if first < split else rest_ref[first - split : end - split]
            part = jnp.dot(weights[:, : end - first], coef, preferred_element_type=jnp.float32)
            acc[:] = part if first == 0 else acc[:] + part

        for g in range(count):
            sun = acc[g * rows : (g + 1) * rows]
            power = jnp.ceil(jnp.log2(jnp.maximum(jnp.max(sun, axis=0, keepdims=True), 1e-30)))
            code = jnp.round(sun * (LEVELS / jnp.exp2(power)) - 0.5 * LEVELS)
            code = code.astype(jnp.int32).astype(jnp.int16)
            cuts = [slice(c, c + LANES) for c in range(0, code.shape[1], LANES)]
            for c, cut in enumerate(cuts):
                outs[g][c * rows : (c + 1) * rows] = code[:, cut]
            tail = [power[:, cut] for cut in cuts] + [jnp.zeros((TAIL - len(cuts), LANES), jnp.float32)]
            outs[g][len(cuts) * rows :] = jnp.concatenate(tail, axis=0).astype(jnp.int32).astype(jnp.int16)

    return kernel


def base_kernel(
    token, sky_hbm, open_hbm, closed_hbm, target_hbm, cross_ref, closed_out, target_out, sky_ref, open_ref, closed_ref, sems
):
    pairs = [(sky_hbm, sky_ref), (open_hbm, open_ref), (closed_hbm, closed_ref), (target_hbm, target_out)]
    copies = fetch(pairs, sems)
    for c in copies[:3]:
        c.wait()
    over = (((0,), (0,)), ((), ()))
    closed = lax.dot_general(sky_ref[:], closed_ref[:], over, preferred_element_type=jnp.float32)
    opened = lax.dot_general(sky_ref[:], open_ref[:], over, preferred_element_type=jnp.float32)
    closed_out[:] = closed
    cross_ref[:] = opened - closed
    copies[3].wait()


def place(me_ref, mask, width):
    return pl.ds(pl.multiple_of((me_ref[0] ^ mask) * width, LANES), width)


def cross_of(codes, base):
    rows, width = base.shape
    columns = width // LANES
    scales = jnp.exp2(codes[columns * rows :].astype(jnp.int32).astype(jnp.float32)) / LEVELS
    suns = []
    for c in range(columns):
        code = codes[c * rows : (c + 1) * rows].astype(jnp.int32).astype(jnp.float32)
        suns.append((code + 0.5 * LEVELS) * scales[c : c + 1])
    return base + jnp.concatenate(suns, axis=1)


def grad_terms(me_ref, base_ref, closed_ref, target_ref, codes, masks, linear, square):
    rows, width = base_ref.shape[0], linear.shape[1]
    for mask, code in zip(masks, codes):
        at = place(me_ref, mask, width)
        cross = cross_of(code, base_ref[:, at])
        apart = closed_ref[:, at] - target_ref[:, at].astype(jnp.float32)
        linear = linear + jnp.sum((apart * cross).reshape(rows // 8, 8, width), axis=0)
        square = square + jnp.sum((cross * cross).reshape(rows // 8, 8, width), axis=0)
    return linear, square


def first_kernel(masks):
    def kernel(me_ref, base_ref, closed_ref, target_ref, *refs):
        codes, out_ref = refs[:-1], refs[-1]
        zero = jnp.zeros(out_ref.shape[1:], jnp.float32)
        out_ref[0], out_ref[1] = grad_terms(me_ref, base_ref, closed_ref, target_ref, codes, masks, zero, zero)

    return kernel


def second_kernel(masks, zones):
    def kernel(me_ref, own_ref, base_ref, closed_ref, target_ref, first_ref, sums_ref, *refs):
        codes, out_ref = refs[:-1], refs[-1]
        linear, square = grad_terms(
            me_ref, base_ref, closed_ref, target_ref, codes, masks, first_ref[0], first_ref[1]
        )
        lane = lax.broadcasted_iota(jnp.int32, sums_ref.shape, 1)
        row = jnp.where(lane == own_ref[0], 2.0 * jnp.sum(linear, keepdims=True), sums_ref[:])
        row = jnp.where(lane == own_ref[0] + zones, 2.0 * jnp.sum(square, keepdims=True), row)
        out_ref[:] = jnp.broadcast_to(row[None], out_ref.shape)

    return kernel


def last_kernel(groups, zones, windows):
    def kernel(place_ref, own_ref, heard_ref, zone_ref, area_ref, openness_ref, base_ref, closed_ref, *refs):
        codes, (lit_ref, step_ref) = refs[:groups], refs[groups:]
        total = jnp.sum(heard_ref[:], axis=0)
        linear, quadratic, num, den, squares = [total[:, i * zones : (i + 1) * zones] for i in range(5)]
        share = num / den
        lane = lax.broadcasted_iota(jnp.int32, share.shape, 1)
        own_share = jnp.sum(jnp.where(lane == own_ref[0], share, 0.0), keepdims=True)
        width = closed_ref.shape[1] // groups
        for mask in range(groups):
            at = place(place_ref, mask, width)
            lit = closed_ref[:, at] + own_share * cross_of(codes[mask], base_ref[:, at])
            lit_ref[:, at] = lit.astype(jnp.bfloat16)
        ratio = groups * (linear + share * quadratic) / den
        rms = jnp.sqrt(jnp.sum(ratio * ratio * squares, keepdims=True) / (windows * groups) + 1e-06)
        zone = zone_ref[:]
        chosen = jnp.zeros(zone.shape, jnp.float32)
        for z in range(zones):
            chosen = jnp.where(zone == z, ratio[:, z : z + 1], chosen)
        step_ref[:] = jnp.clip(openness_ref[:] - 0.25 * (area_ref[:] * chosen) / rms, 0.0, 1.0)

    return kernel


def local(sky, sky_open, sky_closed, sun_coef, sun_bins, sun_rad, target, zone_of, area, openness):
    zones = lax.axis_size("sens")
    groups = lax.axis_size("hour")
    me = lax.axis_index("hour").astype(jnp.int32)[None]
    own_zone = lax.axis_index("sens").astype(jnp.int32)[None]
    rows, patches = sky.shape
    kbins = sun_bins.shape[1]
    nbins, width = sun_coef.shape
    hours = rows * groups
    sensors = groups * width
    windows = area.shape[0]
    assert nbins % LANES == 0 or nbins % LANES >= 2 * kbins
    assert nbins <= 256 * LANES and width % LANES == 0 and windows % LANES == 0 and 3 * kbins <= HEAD
    assert groups == 4 and rows % 16 == 0
    shape = jax.ShapeDtypeStruct
    f32, bf16 = jnp.float32, jnp.bfloat16
    dma = lambda n: pltpu.SemaphoreType.DMA((n,))

    packed = call(
        pack_kernel,
        "pack",
        shape((HEAD, rows), bf16),
        in_specs=[HBM, HBM],
        scratch_shapes=[pltpu.VMEM((kbins, rows), jnp.int32), pltpu.VMEM((kbins, rows), bf16), dma(2)],
    )(sun_bins.T, sun_rad.T)
    heads = {mask: exchange(packed, "hour", mask) for mask in (2, 1, 3)} | {0: packed}

    tiles = (windows // LANES, LANES)
    message = pl.cdiv(5 * zones, LANES) * LANES
    split = nbins // 2 // (CHUNK * LANES) * CHUNK * LANES + CHUNK * LANES
    assert split + 2 * CHUNK * LANES < nbins <= split + 3 * CHUNK * LANES
    coef, zone_sums, zone2, area2, openness2 = call(
        fetch_kernel(zones),
        "fetch",
        [shape((split, width), bf16), shape((1, message), f32)]
        + [shape(tiles, jnp.int32), shape(tiles, f32), shape(tiles, f32)],
        in_specs=[HBM] * 4,
        out_specs=[VMEM] * 5,
        scratch_shapes=[dma(4)],
    )(sun_coef, zone_of.reshape(tiles), area.reshape(tiles), openness.reshape(tiles))

    assert width // LANES <= TAIL

    def sun(masks, rest, stream):
        count = len(masks)
        late = [shape((nbins - split, width), bf16)] if stream else []
        scratch = [pltpu.VMEM((count * rows, width), f32)] + [pltpu.VMEM((count * rows, LANES), PATTERN)] * 2
        return call(
            sun_kernel(count, kbins, stream),
            "sun",
            [shape((width // LANES * rows + TAIL, LANES), jnp.int16)] * count + late,
            in_specs=[VMEM, HBM if stream else VMEM] + [VMEM] * count,
            out_specs=[VMEM] * (count + len(late)),
            scratch_shapes=scratch + ([dma(2)] if stream else []),
        )(coef, rest, *[heads[mask] for mask in masks])

    codes = [None] * groups
    codes[2], late = sun([2], sun_coef, True)
    codes[1], codes[3] = sun([1, 3], late, False)
    (codes[0],) = sun([0], late, False)
    codes = [exchange(code, "hour", mask) if mask else code for mask, code in enumerate(codes)]

    base, closed, wanted = call(
        base_kernel,
        "base",
        [shape((rows, sensors), f32)] * 2 + [shape((rows, sensors), bf16)],
        in_specs=[ANY] + [HBM] * 4,
        out_specs=[VMEM] * 3,
        scratch_shapes=[
            pltpu.VMEM((patches, rows), bf16),
            pltpu.VMEM((patches, sensors), bf16),
            pltpu.VMEM((patches, sensors), bf16),
            dma(4),
        ],
    )(codes[0], sky.T, sky_open, sky_closed, target)
    first, second = [2, 0], [1, 3]
    first_sums = call(
        first_kernel(first),
        "first",
        shape((2, 8, width), f32),
        in_specs=[SMEM] + [VMEM] * (3 + len(first)),
    )(me, base, closed, wanted, *[codes[mask] for mask in first])
    sent = call(
        second_kernel(second, zones),
        "second",
        shape((zones * groups, 1, message), f32),
        in_specs=[SMEM] * 2 + [VMEM] * (5 + len(second)),
    )(me, own_zone, base, closed, wanted, first_sums, zone_sums, *[codes[mask] for mask in second])
    heard = lax.all_to_all(sent, ("sens", "hour"), 0, 0)
    illuminance, new_openness = call(
        last_kernel(groups, zones, windows * zones),
        "last",
        [shape((rows, sensors), bf16), shape(tiles, f32)],
        in_specs=[SMEM] * 2 + [VMEM] * (6 + groups),
    )(me, own_zone, heard, zone2, area2, openness2, base, closed, *codes)
    return (illuminance, new_openness.reshape(-1))


def solution(mesh):
    in_specs = (
        P("hour", None),
        P(None, "sens"),
        P(None, "sens"),
        P(None, ("sens", "hour")),
        P("hour", None),
        P("hour", None),
        P("hour", "sens"),
        P("sens", None),
        P("sens"),
        P("sens"),
    )
    out_specs = (P("hour", "sens"), P("sens"))
    return jax.shard_map(local, mesh=mesh, in_specs=in_specs, out_specs=out_specs, check_vma=False)
```

profile of v0, /device:TPU:0, one launch (start us, length us, event | category | flops | bytes accessed | tf_op | source)
XLA Modules:
  0.0 41.1 jit_solution(12002505292041567140)
XLA Ops:
  0.6 0.7 %pack.1.refs_0_ = bf16[16,128]{1,0:T(8,128)(2,1)S(1)} custom-call(s32[4,128]{1,0:T(4,128)} %bitcast.13, bf16[4,128]{1,0:T(4,128)(2,1)} %bitcast.14), custom_call_target="tpu_custom_call" | custom-call | tf_op jit(solution)/shard_map/pack/pallas_call | solution.py:31
  1.4 4.1 %collective-permute-start = (bf16[16,128]{1,0:T(8,128)(2,1)S(1)}, bf16[16,128]{1,0:T(8,128)(2,1)S(1)}, u32[]{:S(2)}, u32[]{:S(2)}) collective-permute-start(bf16[16,128]{1,0:T(8,128)(2,1)S(1)} %pack.1.refs_0_), channel_id=1, source_target_pairs={{0,2},{1,3},{2,0},{3,1},{4,6},{5,7},{6,4},{7,5},{8,10},{9,11},{10,... | collective-permute-start | bytes 12296 | tf_op jit(solution)/shard_map/ppermute | solution.py:37
  5.5 1.3 %collective-permute-start.3 = (bf16[16,128]{1,0:T(8,128)(2,1)S(1)}, bf16[16,128]{1,0:T(8,128)(2,1)S(1)}, u32[]{:S(2)}, u32[]{:S(2)}) collective-permute-start(bf16[16,128]{1,0:T(8,128)(2,1)S(1)} %pack.1.refs_0_), channel_id=1, source_target_pairs={{0,3},{1,2},{2,1},{3,0},{4,7},{5,6},{6,5},{7,4},{8,11},{9,10},{10,... | collective-permute-start | bytes 12296 | tf_op jit(solution)/shard_map/ppermute | solution.py:37
  6.8 0.2 collective-permute-start.2
  7.0 2.0 %fetch.1 = (bf16[3072,512]{1,0:T(8,128)(2,1)S(1)}, f32[1,128]{1,0:T(1,128)S(1)}, s32[8,128]{1,0:T(8,128)S(1)}, f32[8,128]{1,0:T(8,128)S(1)}, f32[8,128]{1,0:T(8,128)S(1)}) custom-call(bf16[5165,512]{1,0:T(8,128)(2,1)} %rest_in.1, s32[8,128]{1,0:T(8,128)} %bitcast.10, f32[8,128]{1,0:T(8,128)} %bitcast.11, f32[8,128]{1,0:T(8,128)} %bitcast.12), custom_call_target="tpu_custom_call" | custom-call | tf_op jit(solution)/shard_map/fetch/pallas_call | solution.py:31
  9.0 0.0 copy-start.2
  9.0 0.6 %copy-done.2 = s32[8,128]{1,0:T(8,128)} copy-done((s32[8,128]{1,0:T(8,128)}, s32[8,128]{1,0:T(8,128)S(1)}, u32[]{:S(2)}) %copy-start.2) | copy-done | bytes 4120
  9.6 0.6 %copy-done.4 = f32[8,128]{1,0:T(8,128)} copy-done((f32[8,128]{1,0:T(8,128)}, f32[8,128]{1,0:T(8,128)S(1)}, u32[]{:S(2)}) %copy-start.4) | copy-done | bytes 4120
  10.2 2.8 %sun.3 = (s16[520,128]{1,0:T(8,128)(2,1)}, bf16[2093,512]{1,0:T(8,128)(2,1)S(1)}) custom-call(bf16[3072,512]{1,0:T(8,128)(2,1)S(1)} %get-tuple-element.16.first_ref, bf16[5165,512]{1,0:T(8,128)(2,1)} %rest_in.1, bf16[16,128]{1,0:T(8,128)(2,1)S(1)} %collective-permute-done.refs_0_), custom_call_target="tpu_custom_call" | custom-call | tf_op jit(solution)/shard_map/sun/pallas_call | solution.py:31
  13.0 2.9 %collective-permute-start.1 = (s16[520,128]{1,0:T(8,128)(2,1)}, s16[520,128]{1,0:T(8,128)(2,1)S(1)}, u32[]{:S(2)}, u32[]{:S(2)}) collective-permute-start(s16[520,128]{1,0:T(8,128)(2,1)} %get-tuple-element.21), channel_id=1, source_target_pairs={{0,2},{1,3},{2,0},{3,1},{4,6},{5,7},{6,4},{7,5},{8,10},{9,11},{10,... | collective-permute-start | bytes 399368 | tf_op jit(solution)/shard_map/ppermute | solution.py:37
  15.9 2.9 %sun.5 = (s16[520,128]{1,0:T(8,128)(2,1)}, s16[520,128]{1,0:T(8,128)(2,1)}) custom-call(bf16[3072,512]{1,0:T(8,128)(2,1)S(1)} %get-tuple-element.16.first_ref, bf16[2093,512]{1,0:T(8,128)(2,1)S(1)} %get-tuple-element.17.rest_in, bf16[16,128]{1,0:T(8,128)(2,1)S(1)} %collective-permute-done.2.refs_0_, bf16[16,128]{1,0:T(8,128)(2,1)S(1)} %collective-permute-done.3.refs_1_), custom_call_target="tpu_custom_call" | custom-call | tf_op jit(solution)/shard_map/sun/pallas_call | solution.py:31
  18.8 1.3 %copy-done = bf16[2093,512]{1,0:T(8,128)(2,1)} copy-done((bf16[2093,512]{1,0:T(8,128)(2,1)}, bf16[2093,512]{1,0:T(8,128)(2,1)S(1)}, u32[]{:S(2)}) %copy-start) | copy-done | bytes 2143256
  20.1 0.7 %collective-permute-start.4 = (s16[520,128]{1,0:T(8,128)(2,1)}, s16[520,128]{1,0:T(8,128)(2,1)S(1)}, u32[]{:S(2)}, u32[]{:S(2)}) collective-permute-start(s16[520,128]{1,0:T(8,128)(2,1)} %get-tuple-element.23), channel_id=1, source_target_pairs={{0,1},{1,0},{2,3},{3,2},{4,5},{5,4},{6,7},{7,6},{8,9},{9,8},{10,11... | collective-permute-start | bytes 399368 | tf_op jit(solution)/shard_map/ppermute | solution.py:37
  20.8 0.9 %collective-permute-start.5 = (s16[520,128]{1,0:T(8,128)(2,1)}, s16[520,128]{1,0:T(8,128)(2,1)S(1)}, u32[]{:S(2)}, u32[]{:S(2)}) collective-permute-start(s16[520,128]{1,0:T(8,128)(2,1)} %get-tuple-element.24), channel_id=1, source_target_pairs={{0,3},{1,2},{2,1},{3,0},{4,7},{5,6},{6,5},{7,4},{8,11},{9,10},{10,... | collective-permute-start | bytes 399368 | tf_op jit(solution)/shard_map/ppermute | solution.py:37
  21.7 1.6 %copy-done.1 = bf16[2093,512]{1,0:T(8,128)(2,1)S(1)} copy-done((bf16[2093,512]{1,0:T(8,128)(2,1)S(1)}, bf16[2093,512]{1,0:T(8,128)(2,1)}, u32[]{:S(2)}) %copy-start.1) | copy-done | bytes 2143256
  23.3 1.3 %sun.4.token.refs_1_.refs_0_ = s16[520,128]{1,0:T(8,128)(2,1)S(1)} custom-call(bf16[3072,512]{1,0:T(8,128)(2,1)S(1)} %get-tuple-element.16.first_ref, bf16[2093,512]{1,0:T(8,128)(2,1)S(1)} %copy-done.1, bf16[16,128]{1,0:T(8,128)(2,1)S(1)} %pack.1.refs_0_), custom_call_target="tpu_custom_call" | custom-call | tf_op jit(solution)/shard_map/sun/pallas_call | solution.py:31
  24.7 1.8 %base.1 = (f32[128,2048]{1,0:T(8,128)S(1)}, f32[128,2048]{1,0:T(8,128)S(1)}, bf16[128,2048]{1,0:T(8,128)(2,1)S(1)}) custom-call(s16[520,128]{1,0:T(8,128)(2,1)S(1)} %sun.4.token.refs_1_.refs_0_, bf16[146,128]{1,0:T(8,128)(2,1)} %bitcast.9, bf16[146,2048]{1,0:T(8,128)(2,1)} %open_hbm.1, bf16[146,2048]{1,0:T(8,128)(2,1)} %closed_hbm.1, ...), custom_call_target="tpu_custom_call" | custom-call | tf_op jit(solution)/shard_map/base/pallas_call | solution.py:31
  26.5 0.0 copy-start.3
  26.5 0.0 collective-permute-done.1.refs_0_.refs_2_
  26.5 0.3 first.1.first_ref
  26.8 1.4 %collective-permute-done.4.refs_0_.refs_1_ = s16[520,128]{1,0:T(8,128)(2,1)S(1)} collective-permute-done((s16[520,128]{1,0:T(8,128)(2,1)}, s16[520,128]{1,0:T(8,128)(2,1)S(1)}, u32[]{:S(2)}, u32[]{:S(2)}) %collective-permute-start.4) | collective-permute-done | bytes 133152 | tf_op jit(solution)/shard_map/ppermute | solution.py:37
  28.2 0.4 second.1
  28.6 11.2 %all_to_all.5.heard_ref = f32[32,1,128]{2,1,0:T(1,128)S(1)} all-to-all(f32[32,1,128]{2,1,0:T(1,128)S(1)} %second.1), channel_id=1, replica_groups=mesh['sens'=8,'hour'=4] {'sens','hour'}, dimensions={0} | all-to-all | bytes 32768 | tf_op jit(solution)/shard_map/all_to_all | solution.py:316
  39.7 1.4 %last.1 = (bf16[128,2048]{1,0:T(8,128)(2,1)}, f32[8,128]{1,0:T(8,128)}) custom-call(s32[1]{0:T(128)} %bitcast.me_ref.place_ref, s32[1]{0:T(128)} %bitcast.1.own_ref, f32[32,1,128]{2,1,0:T(1,128)S(1)} %all_to_all.5.heard_ref, s32[8,128]{1,0:T(8,128)S(1)} %copy-done.3, f32[8,128]{1,0:T(8,128)S(1)} %copy-done.5, f32[8,128]{1,0:T(8,128)S(1)} %copy-done.7, ...), custom_call_target="tpu_custom_call" | custom-call | tf_op jit(solution)/shard_map/last/pallas_call | solution.py:31
  (18 shorter events, 0.0 us)
Async XLA Ops:
  1.4 8.9 %collective-permute-start = (bf16[16,128]{1,0:T(8,128)(2,1)S(1)}, bf16[16,128]{1,0:T(8,128)(2,1)S(1)}, u32[]{:S(2)}, u32[]{:S(2)}) collective-permute-start(bf16[16,128]{1,0:T(8,128)(2,1)S(1)} %pack.1.refs_0_), channel_id=1, source_target_pairs={{0,2},{1,3},{2,0},{3,1},{4,6},{5,7},{6,4},{7,5},{8,10},{9,11},{10,... | collective-permute-start | bytes 12296 | tf_op jit(solution)/shard_map/ppermute | solution.py:37
  5.5 10.4 %collective-permute-start.3 = (bf16[16,128]{1,0:T(8,128)(2,1)S(1)}, bf16[16,128]{1,0:T(8,128)(2,1)S(1)}, u32[]{:S(2)}, u32[]{:S(2)}) collective-permute-start(bf16[16,128]{1,0:T(8,128)(2,1)S(1)} %pack.1.refs_0_), channel_id=1, source_target_pairs={{0,3},{1,2},{2,1},{3,0},{4,7},{5,6},{6,5},{7,4},{8,11},{9,10},{10,... | collective-permute-start | bytes 12296 | tf_op jit(solution)/shard_map/ppermute | solution.py:37
  6.8 9.1 %collective-permute-start.2 = (bf16[16,128]{1,0:T(8,128)(2,1)S(1)}, bf16[16,128]{1,0:T(8,128)(2,1)S(1)}, u32[]{:S(2)}, u32[]{:S(2)}) collective-permute-start(bf16[16,128]{1,0:T(8,128)(2,1)S(1)} %pack.1.refs_0_), channel_id=1, source_target_pairs={{0,1},{1,0},{2,3},{3,2},{4,5},{5,4},{6,7},{7,6},{8,9},{9,8},{10,11... | collective-permute-start | bytes 12296 | tf_op jit(solution)/shard_map/ppermute | solution.py:37
  9.0 0.6 %copy-start.2 = (s32[8,128]{1,0:T(8,128)}, s32[8,128]{1,0:T(8,128)S(1)}, u32[]{:S(2)}) copy-start(s32[8,128]{1,0:T(8,128)S(1)} %get-tuple-element.25.zone_ref) | copy-start | bytes 12292
  9.6 0.6 %copy-start.4 = (f32[8,128]{1,0:T(8,128)}, f32[8,128]{1,0:T(8,128)S(1)}, u32[]{:S(2)}) copy-start(f32[8,128]{1,0:T(8,128)S(1)} %get-tuple-element.26.area_ref) | copy-start | bytes 12292
  10.2 2.8 %copy-start.6 = (f32[8,128]{1,0:T(8,128)}, f32[8,128]{1,0:T(8,128)S(1)}, u32[]{:S(2)}) copy-start(f32[8,128]{1,0:T(8,128)S(1)} %get-tuple-element.27.openness_ref) | copy-start | bytes 12292
  10.2 2.8 %copy-start.8 = (f32[1,128]{1,0:T(1,128)}, f32[1,128]{1,0:T(1,128)S(1)}, u32[]{:S(2)}) copy-start(f32[1,128]{1,0:T(1,128)S(1)} %get-tuple-element.22.sums_ref) | copy-start | bytes 1540
  13.0 13.5 %collective-permute-start.1 = (s16[520,128]{1,0:T(8,128)(2,1)}, s16[520,128]{1,0:T(8,128)(2,1)S(1)}, u32[]{:S(2)}, u32[]{:S(2)}) collective-permute-start(s16[520,128]{1,0:T(8,128)(2,1)} %get-tuple-element.21), channel_id=1, source_target_pairs={{0,2},{1,3},{2,0},{3,1},{4,6},{5,7},{6,4},{7,5},{8,10},{9,11},{10,... | collective-permute-start | bytes 399368 | tf_op jit(solution)/shard_map/ppermute | solution.py:37
  18.8 1.3 %copy-start = (bf16[2093,512]{1,0:T(8,128)(2,1)}, bf16[2093,512]{1,0:T(8,128)(2,1)S(1)}, u32[]{:S(2)}) copy-start(bf16[2093,512]{1,0:T(8,128)(2,1)S(1)} %get-tuple-element.17.rest_in) | copy-start | bytes 6429700
  20.1 8.0 %collective-permute-start.4 = (s16[520,128]{1,0:T(8,128)(2,1)}, s16[520,128]{1,0:T(8,128)(2,1)S(1)}, u32[]{:S(2)}, u32[]{:S(2)}) collective-permute-start(s16[520,128]{1,0:T(8,128)(2,1)} %get-tuple-element.23), channel_id=1, source_target_pairs={{0,1},{1,0},{2,3},{3,2},{4,5},{5,4},{6,7},{7,6},{8,9},{9,8},{10,11... | collective-permute-start | bytes 399368 | tf_op jit(solution)/shard_map/ppermute | solution.py:37
  20.8 7.4 %collective-permute-start.5 = (s16[520,128]{1,0:T(8,128)(2,1)}, s16[520,128]{1,0:T(8,128)(2,1)S(1)}, u32[]{:S(2)}, u32[]{:S(2)}) collective-permute-start(s16[520,128]{1,0:T(8,128)(2,1)} %get-tuple-element.24), channel_id=1, source_target_pairs={{0,3},{1,2},{2,1},{3,0},{4,7},{5,6},{6,5},{7,4},{8,11},{9,10},{10,... | collective-permute-start | bytes 399368 | tf_op jit(solution)/shard_map/ppermute | solution.py:37
  21.7 1.6 %copy-start.1 = (bf16[2093,512]{1,0:T(8,128)(2,1)S(1)}, bf16[2093,512]{1,0:T(8,128)(2,1)}, u32[]{:S(2)}) copy-start(bf16[2093,512]{1,0:T(8,128)(2,1)} %copy-done) | copy-start | bytes 6429700
  24.7 3.5 %copy-start.9 = (f32[1,128]{1,0:T(1,128)S(1)}, f32[1,128]{1,0:T(1,128)}, u32[]{:S(2)}) copy-start(f32[1,128]{1,0:T(1,128)} %copy-done.8) | copy-start | bytes 1540
  26.5 13.3 %copy-start.3 = (s32[8,128]{1,0:T(8,128)S(1)}, s32[8,128]{1,0:T(8,128)}, u32[]{:S(2)}) copy-start(s32[8,128]{1,0:T(8,128)} %copy-done.2) | copy-start | bytes 12292
  26.5 13.3 %copy-start.5 = (f32[8,128]{1,0:T(8,128)S(1)}, f32[8,128]{1,0:T(8,128)}, u32[]{:S(2)}) copy-start(f32[8,128]{1,0:T(8,128)} %copy-done.4) | copy-start | bytes 12292
  26.5 13.3 %copy-start.7 = (f32[8,128]{1,0:T(8,128)S(1)}, f32[8,128]{1,0:T(8,128)}, u32[]{:S(2)}) copy-start(f32[8,128]{1,0:T(8,128)} %copy-done.6) | copy-start | bytes 12292
where the time goes:
time: 41.4 us; the launch traced here: 41.1 us
  Pallas kernels  13.5 us (33%)
  blocking collectives  11.2 us (27%)
  starting transfers between devices  10.1 us (24%)
  local copies, waits for them, and re-layouts  4.15 us (10%)
  waiting for transfers between devices  1.43 us (3%)
  between operations  0.76 us (2%)
    pallas_call x9, Pallas kernels, call(): run(*[pltpu.with_memory_space_constraint(x, pltpu.HBM) if s is HBM else x...  13.5 us
    all_to_all x1, blocking collectives, local(): heard = lax.all_to_all(sent, ('sens', 'hour'), 0, 0)  11.2 us
    ppermute x6, starting transfers between devices, exchange(): lax.ppermute(x, axis, [(i, i ^ mask) for i in range(lax.axis_size(axis))])  10.1 us
    unnamed x20, local copies, waits for them, and re-layouts  4.15 us
    ppermute x6, waiting for transfers between devices, exchange(): lax.ppermute(x, axis, [(i, i ^ mask) for i in range(lax.axis_size(axis))])  1.43 us
  transfers between devices with their start and end apart: 6, of which 1 were waited for; matrix products, arithmetic and copies ran while one was open for 0% of the time, Pallas kernels for 27%

commit v1 on v0

--- a/solution.py
+++ b/solution.py
@@ -44,7 +44,7 @@
     return copies
 
 
-def pack_kernel(bins_hbm, rad_hbm, out_ref, bins_ref, rad_ref, sems):
+def pack_kernel(me_ref, own_ref, bins_hbm, rad_hbm, out_ref, bins_ref, rad_ref, sems):
     for c in fetch([(bins_hbm, bins_ref), (rad_hbm, rad_ref)], sems):
         c.wait()
     bins = bins_ref[:]
@@ -247,9 +247,9 @@
         pack_kernel,
         "pack",
         shape((HEAD, rows), bf16),
-        in_specs=[HBM, HBM],
+        in_specs=[SMEM, SMEM, HBM, HBM],
         scratch_shapes=[pltpu.VMEM((kbins, rows), jnp.int32), pltpu.VMEM((kbins, rows), bf16), dma(2)],
-    )(sun_bins.T, sun_rad.T)
+    )(me, own_zone, sun_bins.T, sun_rad.T)
     heads = {mask: exchange(packed, "hour", mask) for mask in (2, 1, 3)} | {0: packed}
 
     tiles = (windows // LANES, LANES)

time: 41.4 us -> 38.3 us (0.925)
  local copies, waits for them, and re-layouts: 4.15 us -> 0 us
  waiting for transfers between devices: 1.43 us -> 3.32 us
  Pallas kernels: 13.5 us -> 12 us
  blocking collectives: 11.2 us -> 11.8 us
    unnamed x20 -> x0, local copies, waits for them, and re-layouts: 4.15 us -> none
    ppermute x6, waiting for transfers between devices: 1.43 us -> 3.32 us  [exchange(): lax.ppermute(x, axis, [(i, i ^ mask) for i in range(lax.axis_size(axis))])]
    pallas_call x9, Pallas kernels: 13.5 us -> 12 us  [call(): run(*[pltpu.with_memory_space_constraint(x, pltpu.HBM) if s is HBM else x...]
    all_to_all x1, blocking collectives: 11.2 us -> 11.8 us  [local(): heard = lax.all_to_all(sent, ('sens', 'hour'), 0, 0)]
  transfers between devices with their start and end apart: 6 -> 6, of which waited for: 1 -> 1; matrix products, arithmetic and copies ran while one was open for 0% -> 0% of each run, Pallas kernels for 27% -> 25%
where the time goes in v1:
time: 38.3 us; the launch traced here: 38 us
  Pallas kernels  12 us (31%)
  blocking collectives  11.8 us (31%)
  starting transfers between devices  10.2 us (27%)
  waiting for transfers between devices  3.32 us (9%)
  between operations  0.71 us (2%)
    pallas_call x9, Pallas kernels, call(): run(*[pltpu.with_memory_space_constraint(x, pltpu.HBM) if s is HBM else x...  12 us
    all_to_all x1, blocking collectives, local(): heard = lax.all_to_all(sent, ('sens', 'hour'), 0, 0)  11.8 us
    ppermute x6, starting transfers between devices, exchange(): lax.ppermute(x, axis, [(i, i ^ mask) for i in range(lax.axis_size(axis))])  10.2 us
    ppermute x6, waiting for transfers between devices, exchange(): lax.ppermute(x, axis, [(i, i ^ mask) for i in range(lax.axis_size(axis))])  3.32 us
  transfers between devices with their start and end apart: 6, of which 1 were waited for; matrix products, arithmetic and copies ran while one was open for 0% of the time, Pallas kernels for 25%

profile of v1, /device:TPU:0, one launch (start us, length us, event | category | flops | bytes accessed | tf_op | source)
XLA Modules:
  0.0 38.0 jit_solution(18459596287206583)
XLA Ops:
  0.6 0.7 %pack.1.refs_0_ = bf16[16,128]{1,0:T(8,128)(2,1)S(1)} custom-call(s32[1]{0:T(128)} %bitcast.me_ref.place_ref, s32[1]{0:T(128)} %bitcast.1.own_ref, s32[4,128]{1,0:T(4,128)} %bitcast.13, bf16[4,128]{1,0:T(4,128)(2,1)} %bitcast.14), custom_call_target="tpu_custom_call" | custom-call | tf_op jit(solution)/shard_map/pack/pallas_call | solution.py:31
  1.4 4.1 %collective-permute-start = (bf16[16,128]{1,0:T(8,128)(2,1)S(1)}, bf16[16,128]{1,0:T(8,128)(2,1)S(1)}, u32[]{:S(2)}, u32[]{:S(2)}) collective-permute-start(bf16[16,128]{1,0:T(8,128)(2,1)S(1)} %pack.1.refs_0_), channel_id=1, source_target_pairs={{0,2},{1,3},{2,0},{3,1},{4,6},{5,7},{6,4},{7,5},{8,10},{9,11},{10,... | collective-permute-start | bytes 12296 | tf_op jit(solution)/shard_map/ppermute | solution.py:37
  5.5 1.3 %collective-permute-start.3 = (bf16[16,128]{1,0:T(8,128)(2,1)S(1)}, bf16[16,128]{1,0:T(8,128)(2,1)S(1)}, u32[]{:S(2)}, u32[]{:S(2)}) collective-permute-start(bf16[16,128]{1,0:T(8,128)(2,1)S(1)} %pack.1.refs_0_), channel_id=1, source_target_pairs={{0,3},{1,2},{2,1},{3,0},{4,7},{5,6},{6,5},{7,4},{8,11},{9,10},{10,... | collective-permute-start | bytes 12296 | tf_op jit(solution)/shard_map/ppermute | solution.py:37
  6.8 0.2 collective-permute-start.2
  7.0 2.0 %fetch.1 = (bf16[3072,512]{1,0:T(8,128)(2,1)S(1)}, f32[1,128]{1,0:T(1,128)S(1)}, s32[8,128]{1,0:T(8,128)S(1)}, f32[8,128]{1,0:T(8,128)S(1)}, f32[8,128]{1,0:T(8,128)S(1)}) custom-call(bf16[5165,512]{1,0:T(8,128)(2,1)} %rest_in.1, s32[8,128]{1,0:T(8,128)} %bitcast.10, f32[8,128]{1,0:T(8,128)} %bitcast.11, f32[8,128]{1,0:T(8,128)} %bitcast.12), custom_call_target="tpu_custom_call" | custom-call | tf_op jit(solution)/shard_map/fetch/pallas_call | solution.py:31
  9.0 0.0 collective-permute-done.refs_0_
  9.0 2.0 %sun.3 = (s16[520,128]{1,0:T(8,128)(2,1)S(1)}, bf16[2093,512]{1,0:T(8,128)(2,1)S(1)}) custom-call(bf16[3072,512]{1,0:T(8,128)(2,1)S(1)} %get-tuple-element.16.first_ref, bf16[5165,512]{1,0:T(8,128)(2,1)} %rest_in.1, bf16[16,128]{1,0:T(8,128)(2,1)S(1)} %collective-permute-done.refs_0_), custom_call_target="tpu_custom_call" | custom-call | tf_op jit(solution)/shard_map/sun/pallas_call | solution.py:31
  11.0 2.9 %collective-permute-start.1 = (s16[520,128]{1,0:T(8,128)(2,1)S(1)}, s16[520,128]{1,0:T(8,128)(2,1)S(1)}, u32[]{:S(2)}, u32[]{:S(2)}) collective-permute-start(s16[520,128]{1,0:T(8,128)(2,1)S(1)} %get-tuple-element.21), channel_id=1, source_target_pairs={{0,2},{1,3},{2,0},{3,1},{4,6},{5,7},{6,4},{7,5},{8,10},{9,11},{10,... | collective-permute-start | bytes 399368 | tf_op jit(solution)/shard_map/ppermute | solution.py:37
  13.9 0.0 collective-permute-done.3.refs_1_
  13.9 0.0 collective-permute-done.2.refs_0_
  13.9 2.2 %sun.5 = (s16[520,128]{1,0:T(8,128)(2,1)S(1)}, s16[520,128]{1,0:T(8,128)(2,1)S(1)}) custom-call(bf16[3072,512]{1,0:T(8,128)(2,1)S(1)} %get-tuple-element.16.first_ref, bf16[2093,512]{1,0:T(8,128)(2,1)S(1)} %get-tuple-element.17.rest_in, bf16[16,128]{1,0:T(8,128)(2,1)S(1)} %collective-permute-done.2.refs_0_, bf16[16,128]{1,0:T(8,128)(2,1)S(1)} %collective-permute-done.3.refs_1_), custom_call_target="tpu_custom_call" | custom-call | tf_op jit(solution)/shard_map/sun/pallas_call | solution.py:31
  16.2 0.7 %collective-permute-start.4 = (s16[520,128]{1,0:T(8,128)(2,1)S(1)}, s16[520,128]{1,0:T(8,128)(2,1)S(1)}, u32[]{:S(2)}, u32[]{:S(2)}) collective-permute-start(s16[520,128]{1,0:T(8,128)(2,1)S(1)} %get-tuple-element.23), channel_id=1, source_target_pairs={{0,1},{1,0},{2,3},{3,2},{4,5},{5,4},{6,7},{7,6},{8,9},{9,8},{10,11... | collective-permute-start | bytes 399368 | tf_op jit(solution)/shard_map/ppermute | solution.py:37
  16.9 0.9 %collective-permute-start.5 = (s16[520,128]{1,0:T(8,128)(2,1)S(1)}, s16[520,128]{1,0:T(8,128)(2,1)S(1)}, u32[]{:S(2)}, u32[]{:S(2)}) collective-permute-start(s16[520,128]{1,0:T(8,128)(2,1)S(1)} %get-tuple-element.24), channel_id=1, source_target_pairs={{0,3},{1,2},{2,1},{3,0},{4,7},{5,6},{6,5},{7,4},{8,11},{9,10},{10,... | collective-permute-start | bytes 399368 | tf_op jit(solution)/shard_map/ppermute | solution.py:37
  17.8 1.3 %sun.4.token.refs_1_.refs_0_ = s16[520,128]{1,0:T(8,128)(2,1)S(1)} custom-call(bf16[3072,512]{1,0:T(8,128)(2,1)S(1)} %get-tuple-element.16.first_ref, bf16[2093,512]{1,0:T(8,128)(2,1)S(1)} %get-tuple-element.17.rest_in, bf16[16,128]{1,0:T(8,128)(2,1)S(1)} %pack.1.refs_0_), custom_call_target="tpu_custom_call" | custom-call | tf_op jit(solution)/shard_map/sun/pallas_call | solution.py:31
  19.1 1.8 %base.1 = (f32[128,2048]{1,0:T(8,128)S(1)}, f32[128,2048]{1,0:T(8,128)S(1)}, bf16[128,2048]{1,0:T(8,128)(2,1)S(1)}) custom-call(s16[520,128]{1,0:T(8,128)(2,1)S(1)} %sun.4.token.refs_1_.refs_0_, bf16[146,128]{1,0:T(8,128)(2,1)} %bitcast.9, bf16[146,2048]{1,0:T(8,128)(2,1)} %open_hbm.1, bf16[146,2048]{1,0:T(8,128)(2,1)} %closed_hbm.1, ...), custom_call_target="tpu_custom_call" | custom-call | tf_op jit(solution)/shard_map/base/pallas_call | solution.py:31
  20.9 0.0 collective-permute-done.1.refs_0_.refs_2_
  20.9 0.3 first.1.first_ref
  21.2 3.3 %collective-permute-done.4.refs_0_.refs_1_ = s16[520,128]{1,0:T(8,128)(2,1)S(1)} collective-permute-done((s16[520,128]{1,0:T(8,128)(2,1)S(1)}, s16[520,128]{1,0:T(8,128)(2,1)S(1)}, u32[]{:S(2)}, u32[]{:S(2)}) %collective-permute-start.4) | collective-permute-done | bytes 133152 | tf_op jit(solution)/shard_map/ppermute | solution.py:37
  24.5 0.0 collective-permute-done.5.refs_1_.refs_3_
  24.5 0.4 second.1
  24.9 11.8 %all_to_all.5.heard_ref = f32[32,1,128]{2,1,0:T(1,128)S(1)} all-to-all(f32[32,1,128]{2,1,0:T(1,128)S(1)} %second.1), channel_id=1, replica_groups=mesh['sens'=8,'hour'=4] {'sens','hour'}, dimensions={0} | all-to-all | bytes 32768 | tf_op jit(solution)/shard_map/all_to_all | solution.py:316
  36.6 1.4 %last.1 = (bf16[128,2048]{1,0:T(8,128)(2,1)}, f32[8,128]{1,0:T(8,128)}) custom-call(s32[1]{0:T(128)} %bitcast.me_ref.place_ref, s32[1]{0:T(128)} %bitcast.1.own_ref, f32[32,1,128]{2,1,0:T(1,128)S(1)} %all_to_all.5.heard_ref, s32[8,128]{1,0:T(8,128)S(1)} %get-tuple-element.25.zone_ref, f32[8,128]{1,0:T(8,128)S(1)} %get-tuple-element.26.area_ref, ...), custom_call_target="tpu_custom_call" | custom-call | tf_op jit(solution)/shard_map/last/pallas_call | solution.py:31
Async XLA Ops:
  1.4 7.7 %collective-permute-start = (bf16[16,128]{1,0:T(8,128)(2,1)S(1)}, bf16[16,128]{1,0:T(8,128)(2,1)S(1)}, u32[]{:S(2)}, u32[]{:S(2)}) collective-permute-start(bf16[16,128]{1,0:T(8,128)(2,1)S(1)} %pack.1.refs_0_), channel_id=1, source_target_pairs={{0,2},{1,3},{2,0},{3,1},{4,6},{5,7},{6,4},{7,5},{8,10},{9,11},{10,... | collective-permute-start | bytes 12296 | tf_op jit(solution)/shard_map/ppermute | solution.py:37
  5.5 8.5 %collective-permute-start.3 = (bf16[16,128]{1,0:T(8,128)(2,1)S(1)}, bf16[16,128]{1,0:T(8,128)(2,1)S(1)}, u32[]{:S(2)}, u32[]{:S(2)}) collective-permute-start(bf16[16,128]{1,0:T(8,128)(2,1)S(1)} %pack.1.refs_0_), channel_id=1, source_target_pairs={{0,3},{1,2},{2,1},{3,0},{4,7},{5,6},{6,5},{7,4},{8,11},{9,10},{10,... | collective-permute-start | bytes 12296 | tf_op jit(solution)/shard_map/ppermute | solution.py:37
  6.8 7.1 %collective-permute-start.2 = (bf16[16,128]{1,0:T(8,128)(2,1)S(1)}, bf16[16,128]{1,0:T(8,128)(2,1)S(1)}, u32[]{:S(2)}, u32[]{:S(2)}) collective-permute-start(bf16[16,128]{1,0:T(8,128)(2,1)S(1)} %pack.1.refs_0_), channel_id=1, source_target_pairs={{0,1},{1,0},{2,3},{3,2},{4,5},{5,4},{6,7},{7,6},{8,9},{9,8},{10,11... | collective-permute-start | bytes 12296 | tf_op jit(solution)/shard_map/ppermute | solution.py:37
  11.0 9.9 %collective-permute-start.1 = (s16[520,128]{1,0:T(8,128)(2,1)S(1)}, s16[520,128]{1,0:T(8,128)(2,1)S(1)}, u32[]{:S(2)}, u32[]{:S(2)}) collective-permute-start(s16[520,128]{1,0:T(8,128)(2,1)S(1)} %get-tuple-element.21), channel_id=1, source_target_pairs={{0,2},{1,3},{2,0},{3,1},{4,6},{5,7},{6,4},{7,5},{8,10},{9,11},{10,... | collective-permute-start | bytes 399368 | tf_op jit(solution)/shard_map/ppermute | solution.py:37
  16.2 8.3 %collective-permute-start.4 = (s16[520,128]{1,0:T(8,128)(2,1)S(1)}, s16[520,128]{1,0:T(8,128)(2,1)S(1)}, u32[]{:S(2)}, u32[]{:S(2)}) collective-permute-start(s16[520,128]{1,0:T(8,128)(2,1)S(1)} %get-tuple-element.23), channel_id=1, source_target_pairs={{0,1},{1,0},{2,3},{3,2},{4,5},{5,4},{6,7},{7,6},{8,9},{9,8},{10,11... | collective-permute-start | bytes 399368 | tf_op jit(solution)/shard_map/ppermute | solution.py:37
  16.9 7.6 %collective-permute-start.5 = (s16[520,128]{1,0:T(8,128)(2,1)S(1)}, s16[520,128]{1,0:T(8,128)(2,1)S(1)}, u32[]{:S(2)}, u32[]{:S(2)}) collective-permute-start(s16[520,128]{1,0:T(8,128)(2,1)S(1)} %get-tuple-element.24), channel_id=1, source_target_pairs={{0,3},{1,2},{2,1},{3,0},{4,7},{5,6},{6,5},{7,4},{8,11},{9,10},{10,... | collective-permute-start | bytes 399368 | tf_op jit(solution)/shard_map/ppermute | solution.py:37

commit v2 on v1

--- a/solution.py
+++ b/solution.py
@@ -75,9 +75,17 @@
     return kernel
 
 
-def sun_kernel(count, kbins, stream):
+def join_kernel(token, one_ref, two_ref, out_ref):
+    out_ref[:HEAD] = one_ref[:]
+    out_ref[HEAD:] = two_ref[:]
+
+
+def sun_kernel(sources, kbins, stream):
+    count = len(sources)
+    inputs = 1 + max(operand for operand, _ in sources)
+
     def kernel(first_ref, rest_in, *refs):
-        heads, outs, rest = refs[:count], refs[count : 2 * count], refs[2 * count :]
+        heads, outs, rest = refs[:inputs], refs[inputs : inputs + count], refs[inputs + count :]
         rows = heads[0].shape[1]
         split = first_ref.shape[0]
         nbins = split + rest_in.shape[0] - (split if stream else 0)
@@ -100,7 +108,8 @@
             waits = {}
         lane = lax.broadcasted_iota(jnp.int32, (rows, LANES), 1)
         for g in range(count):
-            small = heads[g][:].astype(jnp.float32).T
+            operand, offset = sources[g]
+            small = heads[operand][offset : offset + HEAD].astype(jnp.float32).T
             value = jnp.zeros((rows, LANES), jnp.float32)
             where = jnp.zeros((rows, LANES), jnp.float32)
             for k in range(kbins):
@@ -250,12 +259,12 @@
         in_specs=[SMEM, SMEM, HBM, HBM],
         scratch_shapes=[pltpu.VMEM((kbins, rows), jnp.int32), pltpu.VMEM((kbins, rows), bf16), dma(2)],
     )(me, own_zone, sun_bins.T, sun_rad.T)
-    heads = {mask: exchange(packed, "hour", mask) for mask in (2, 1, 3)} | {0: packed}
+    far = exchange(packed, "hour", 2)
 
     tiles = (windows // LANES, LANES)
     message = pl.cdiv(5 * zones, LANES) * LANES
-    split = nbins // 2 // (CHUNK * LANES) * CHUNK * LANES + CHUNK * LANES
-    assert split + 2 * CHUNK * LANES < nbins <= split + 3 * CHUNK * LANES
+    split = (nbins // (CHUNK * LANES) - 1) * CHUNK * LANES
+    assert 0 < split and split + CHUNK * LANES < nbins
     coef, zone_sums, zone2, area2, openness2 = call(
         fetch_kernel(zones),
         "fetch",
@@ -266,25 +275,28 @@
         scratch_shapes=[dma(4)],
     )(sun_coef, zone_of.reshape(tiles), area.reshape(tiles), openness.reshape(tiles))
 
+    both = call(join_kernel, "join", shape((2 * HEAD, rows), bf16), in_specs=[ANY] + [VMEM] * 2)(zone_sums, packed, far)
+    near = exchange(both, "hour", 1)
+
     assert width // LANES <= TAIL
 
-    def sun(masks, rest, stream):
-        count = len(masks)
+    def sun(sources, rest, stream, *heads):
+        count = len(sources)
         late = [shape((nbins - split, width), bf16)] if stream else []
         scratch = [pltpu.VMEM((count * rows, width), f32)] + [pltpu.VMEM((count * rows, LANES), PATTERN)] * 2
         return call(
-            sun_kernel(count, kbins, stream),
+            sun_kernel(sources, kbins, stream),
             "sun",
             [shape((width // LANES * rows + TAIL, LANES), jnp.int16)] * count + late,
-            in_specs=[VMEM, HBM if stream else VMEM] + [VMEM] * count,
+            in_specs=[VMEM, HBM if stream else VMEM] + [VMEM] * len(heads),
             out_specs=[VMEM] * (count + len(late)),
-            scratch_shapes=scratch + ([dma(2)] if stream else []),
-        )(coef, rest, *[heads[mask] for mask in masks])
+            scratch_shapes=scratch + ([dma(1)] if stream else []),
+        )(coef, rest, *heads)
 
     codes = [None] * groups
-    codes[2], late = sun([2], sun_coef, True)
-    codes[1], codes[3] = sun([1, 3], late, False)
-    (codes[0],) = sun([0], late, False)
+    codes[2], late = sun([(0, 0)], sun_coef, True, far)
+    codes[1], codes[3] = sun([(0, 0), (0, HEAD)], late, False, near)
+    (codes[0],) = sun([(0, 0)], late, False, packed)
     codes = [exchange(code, "hour", mask) if mask else code for mask, code in enumerate(codes)]
 
     base, closed, wanted = call(

time: 38.3 us -> 37.1 us (0.969)
  blocking collectives: 11.8 us -> 10.4 us
    all_to_all x1, blocking collectives: 11.8 us -> 10.4 us  [local(): heard = lax.all_to_all(sent, ('sens', 'hour'), 0, 0)]
    ppermute x6 -> x5, waiting for transfers between devices: 3.32 us -> 3.42 us  [exchange(): lax.ppermute(x, axis, [(i, i ^ mask) for i in range(lax.axis_size(axis))])]
    ppermute x6 -> x5, starting transfers between devices: 10.2 us -> 10.3 us  [exchange(): lax.ppermute(x, axis, [(i, i ^ mask) for i in range(lax.axis_size(axis))])]
    pallas_call x9 -> x10, Pallas kernels: 12 us -> 12 us  [call(): run(*[pltpu.with_memory_space_constraint(x, pltpu.HBM) if s is HBM else x...]
  transfers between devices with their start and end apart: 6 -> 5, of which waited for: 1 -> 2; matrix products, arithmetic and copies ran while one was open for 0% -> 0% of each run, Pallas kernels for 25% -> 26%
where the time goes in v2:
time: 37.1 us; the launch traced here: 36.8 us
  Pallas kernels  12 us (32%)
  blocking collectives  10.4 us (28%)
  starting transfers between devices  10.3 us (28%)
  waiting for transfers between devices  3.42 us (9%)
  between operations  0.71 us (2%)
    pallas_call x10, Pallas kernels, call(): run(*[pltpu.with_memory_space_constraint(x, pltpu.HBM) if s is HBM else x...  12 us
    all_to_all x1, blocking collectives, local(): heard = lax.all_to_all(sent, ('sens', 'hour'), 0, 0)  10.4 us
    ppermute x5, starting transfers between devices, exchange(): lax.ppermute(x, axis, [(i, i ^ mask) for i in range(lax.axis_size(axis))])  10.3 us
    ppermute x5, waiting for transfers between devices, exchange(): lax.ppermute(x, axis, [(i, i ^ mask) for i in range(lax.axis_size(axis))])  3.42 us
  transfers between devices with their start and end apart: 5, of which 2 were waited for; matrix products, arithmetic and copies ran while one was open for 0% of the time, Pallas kernels for 26%

profile of v2, /device:TPU:0, one launch (start us, length us, event | category | flops | bytes accessed | tf_op | source)
XLA Modules:
  0.0 36.8 jit_solution(932867503733061170)
XLA Ops:
  0.6 0.7 %pack.1.refs_0_.one_ref = bf16[16,128]{1,0:T(8,128)(2,1)S(1)} custom-call(s32[1]{0:T(128)} %bitcast.me_ref.place_ref, s32[1]{0:T(128)} %bitcast.1.own_ref, s32[4,128]{1,0:T(4,128)} %bitcast.13, bf16[4,128]{1,0:T(4,128)(2,1)} %bitcast.14), custom_call_target="tpu_custom_call" | custom-call | tf_op jit(solution)/shard_map/pack/pallas_call | solution.py:31
  1.4 4.1 %collective-permute-start = (bf16[16,128]{1,0:T(8,128)(2,1)S(1)}, bf16[16,128]{1,0:T(8,128)(2,1)S(1)}, u32[]{:S(2)}, u32[]{:S(2)}) collective-permute-start(bf16[16,128]{1,0:T(8,128)(2,1)S(1)} %pack.1.refs_0_.one_ref), channel_id=1, source_target_pairs={{0,2},{1,3},{2,0},{3,1},{4,6},{5,7},{6,4},{7,5},{8,10},{9,11},{10,... | collective-permute-start | bytes 12296 | tf_op jit(solution)/shard_map/ppermute | solution.py:37
  5.5 2.3 %fetch.1 = (bf16[4096,512]{1,0:T(8,128)(2,1)S(1)}, f32[1,128]{1,0:T(1,128)S(1)}, s32[8,128]{1,0:T(8,128)S(1)}, f32[8,128]{1,0:T(8,128)S(1)}, f32[8,128]{1,0:T(8,128)S(1)}) custom-call(bf16[5165,512]{1,0:T(8,128)(2,1)} %rest_in.1, s32[8,128]{1,0:T(8,128)} %bitcast.10, f32[8,128]{1,0:T(8,128)} %bitcast.11, f32[8,128]{1,0:T(8,128)} %bitcast.12), custom_call_target="tpu_custom_call" | custom-call | tf_op jit(solution)/shard_map/fetch/pallas_call | solution.py:31
  7.7 0.0 collective-permute-done.refs_0_.two_ref
  7.8 1.6 %collective-permute-start.2 = (bf16[32,128]{1,0:T(8,128)(2,1)S(1)}, bf16[32,128]{1,0:T(8,128)(2,1)S(1)}, u32[]{:S(2)}, u32[]{:S(2)}) collective-permute-start(bf16[32,128]{1,0:T(8,128)(2,1)S(1)} %join.1), channel_id=1, source_target_pairs={{0,1},{1,0},{2,3},{3,2},{4,5},{5,4},{6,7},{7,6},{8,9},{9,8},{10,11... | collective-permute-start | bytes 24584 | tf_op jit(solution)/shard_map/ppermute | solution.py:37
  9.4 1.7 %sun.3 = (s16[520,128]{1,0:T(8,128)(2,1)S(1)}, bf16[1069,512]{1,0:T(8,128)(2,1)S(1)}) custom-call(bf16[4096,512]{1,0:T(8,128)(2,1)S(1)} %get-tuple-element.16.first_ref, bf16[5165,512]{1,0:T(8,128)(2,1)} %rest_in.1, bf16[16,128]{1,0:T(8,128)(2,1)S(1)} %collective-permute-done.refs_0_.two_ref), custom_call_target="tpu_custom_call" | custom-call | tf_op jit(solution)/shard_map/sun/pallas_call | solution.py:31
  11.1 2.2 %collective-permute-start.1 = (s16[520,128]{1,0:T(8,128)(2,1)S(1)}, s16[520,128]{1,0:T(8,128)(2,1)S(1)}, u32[]{:S(2)}, u32[]{:S(2)}) collective-permute-start(s16[520,128]{1,0:T(8,128)(2,1)S(1)} %get-tuple-element.21), channel_id=1, source_target_pairs={{0,2},{1,3},{2,0},{3,1},{4,6},{5,7},{6,4},{7,5},{8,10},{9,11},{10,... | collective-permute-start | bytes 399368 | tf_op jit(solution)/shard_map/ppermute | solution.py:37
  13.3 0.0 collective-permute-done.2.refs_0_
  13.3 2.2 %sun.5 = (s16[520,128]{1,0:T(8,128)(2,1)S(1)}, s16[520,128]{1,0:T(8,128)(2,1)S(1)}) custom-call(bf16[4096,512]{1,0:T(8,128)(2,1)S(1)} %get-tuple-element.16.first_ref, bf16[1069,512]{1,0:T(8,128)(2,1)S(1)} %get-tuple-element.17.rest_in, bf16[32,128]{1,0:T(8,128)(2,1)S(1)} %collective-permute-done.2.refs_0_), custom_call_target="tpu_custom_call" | custom-call | tf_op jit(solution)/shard_map/sun/pallas_call | solution.py:31
  15.5 0.5 %collective-permute-start.3 = (s16[520,128]{1,0:T(8,128)(2,1)S(1)}, s16[520,128]{1,0:T(8,128)(2,1)S(1)}, u32[]{:S(2)}, u32[]{:S(2)}) collective-permute-start(s16[520,128]{1,0:T(8,128)(2,1)S(1)} %get-tuple-element.23), channel_id=1, source_target_pairs={{0,1},{1,0},{2,3},{3,2},{4,5},{5,4},{6,7},{7,6},{8,9},{9,8},{10,11... | collective-permute-start | bytes 399368 | tf_op jit(solution)/shard_map/ppermute | solution.py:37
  16.1 1.8 %collective-permute-start.4 = (s16[520,128]{1,0:T(8,128)(2,1)S(1)}, s16[520,128]{1,0:T(8,128)(2,1)S(1)}, u32[]{:S(2)}, u32[]{:S(2)}) collective-permute-start(s16[520,128]{1,0:T(8,128)(2,1)S(1)} %get-tuple-element.24), channel_id=1, source_target_pairs={{0,3},{1,2},{2,1},{3,0},{4,7},{5,6},{6,5},{7,4},{8,11},{9,10},{10,... | collective-permute-start | bytes 399368 | tf_op jit(solution)/shard_map/ppermute | solution.py:37
  17.9 1.3 %sun.4.token.refs_1_.refs_0_ = s16[520,128]{1,0:T(8,128)(2,1)S(1)} custom-call(bf16[4096,512]{1,0:T(8,128)(2,1)S(1)} %get-tuple-element.16.first_ref, bf16[1069,512]{1,0:T(8,128)(2,1)S(1)} %get-tuple-element.17.rest_in, bf16[16,128]{1,0:T(8,128)(2,1)S(1)} %pack.1.refs_0_.one_ref), custom_call_target="tpu_custom_call" | custom-call | tf_op jit(solution)/shard_map/sun/pallas_call | solution.py:31
  19.2 1.8 %base.1 = (f32[128,2048]{1,0:T(8,128)S(1)}, f32[128,2048]{1,0:T(8,128)S(1)}, bf16[128,2048]{1,0:T(8,128)(2,1)S(1)}) custom-call(s16[520,128]{1,0:T(8,128)(2,1)S(1)} %sun.4.token.refs_1_.refs_0_, bf16[146,128]{1,0:T(8,128)(2,1)} %bitcast.9, bf16[146,2048]{1,0:T(8,128)(2,1)} %open_hbm.1, bf16[146,2048]{1,0:T(8,128)(2,1)} %closed_hbm.1, ...), custom_call_target="tpu_custom_call" | custom-call | tf_op jit(solution)/shard_map/base/pallas_call | solution.py:31
  21.0 0.3 collective-permute-done.1.refs_0_.refs_2_
  21.2 0.3 first.1.first_ref
  21.5 3.1 %collective-permute-done.3.refs_0_.refs_1_ = s16[520,128]{1,0:T(8,128)(2,1)S(1)} collective-permute-done((s16[520,128]{1,0:T(8,128)(2,1)S(1)}, s16[520,128]{1,0:T(8,128)(2,1)S(1)}, u32[]{:S(2)}, u32[]{:S(2)}) %collective-permute-start.3) | collective-permute-done | bytes 133152 | tf_op jit(solution)/shard_map/ppermute | solution.py:37
  24.6 0.0 collective-permute-done.4.refs_1_.refs_3_
  24.6 0.4 second.1
  25.0 10.4 %all_to_all.5.heard_ref = f32[32,1,128]{2,1,0:T(1,128)S(1)} all-to-all(f32[32,1,128]{2,1,0:T(1,128)S(1)} %second.1), channel_id=1, replica_groups=mesh['sens'=8,'hour'=4] {'sens','hour'}, dimensions={0} | all-to-all | bytes 32768 | tf_op jit(solution)/shard_map/all_to_all | solution.py:328
  35.4 1.4 %last.1 = (bf16[128,2048]{1,0:T(8,128)(2,1)}, f32[8,128]{1,0:T(8,128)}) custom-call(s32[1]{0:T(128)} %bitcast.me_ref.place_ref, s32[1]{0:T(128)} %bitcast.1.own_ref, f32[32,1,128]{2,1,0:T(1,128)S(1)} %all_to_all.5.heard_ref, s32[8,128]{1,0:T(8,128)S(1)} %get-tuple-element.25.zone_ref, f32[8,128]{1,0:T(8,128)S(1)} %get-tuple-element.26.area_ref, ...), custom_call_target="tpu_custom_call" | custom-call | tf_op jit(solution)/shard_map/last/pallas_call | solution.py:31
  (1 shorter events, 0.0 us)
Async XLA Ops:
  1.4 6.4 %collective-permute-start = (bf16[16,128]{1,0:T(8,128)(2,1)S(1)}, bf16[16,128]{1,0:T(8,128)(2,1)S(1)}, u32[]{:S(2)}, u32[]{:S(2)}) collective-permute-start(bf16[16,128]{1,0:T(8,128)(2,1)S(1)} %pack.1.refs_0_.one_ref), channel_id=1, source_target_pairs={{0,2},{1,3},{2,0},{3,1},{4,6},{5,7},{6,4},{7,5},{8,10},{9,11},{10,... | collective-permute-start | bytes 12296 | tf_op jit(solution)/shard_map/ppermute | solution.py:37
  7.8 5.5 %collective-permute-start.2 = (bf16[32,128]{1,0:T(8,128)(2,1)S(1)}, bf16[32,128]{1,0:T(8,128)(2,1)S(1)}, u32[]{:S(2)}, u32[]{:S(2)}) collective-permute-start(bf16[32,128]{1,0:T(8,128)(2,1)S(1)} %join.1), channel_id=1, source_target_pairs={{0,1},{1,0},{2,3},{3,2},{4,5},{5,4},{6,7},{7,6},{8,9},{9,8},{10,11... | collective-permute-start | bytes 24584 | tf_op jit(solution)/shard_map/ppermute | solution.py:37
  11.1 10.2 %collective-permute-start.1 = (s16[520,128]{1,0:T(8,128)(2,1)S(1)}, s16[520,128]{1,0:T(8,128)(2,1)S(1)}, u32[]{:S(2)}, u32[]{:S(2)}) collective-permute-start(s16[520,128]{1,0:T(8,128)(2,1)S(1)} %get-tuple-element.21), channel_id=1, source_target_pairs={{0,2},{1,3},{2,0},{3,1},{4,6},{5,7},{6,4},{7,5},{8,10},{9,11},{10,... | collective-permute-start | bytes 399368 | tf_op jit(solution)/shard_map/ppermute | solution.py:37
  15.5 9.1 %collective-permute-start.3 = (s16[520,128]{1,0:T(8,128)(2,1)S(1)}, s16[520,128]{1,0:T(8,128)(2,1)S(1)}, u32[]{:S(2)}, u32[]{:S(2)}) collective-permute-start(s16[520,128]{1,0:T(8,128)(2,1)S(1)} %get-tuple-element.23), channel_id=1, source_target_pairs={{0,1},{1,0},{2,3},{3,2},{4,5},{5,4},{6,7},{7,6},{8,9},{9,8},{10,11... | collective-permute-start | bytes 399368 | tf_op jit(solution)/shard_map/ppermute | solution.py:37
  16.1 8.6 %collective-permute-start.4 = (s16[520,128]{1,0:T(8,128)(2,1)S(1)}, s16[520,128]{1,0:T(8,128)(2,1)S(1)}, u32[]{:S(2)}, u32[]{:S(2)}) collective-permute-start(s16[520,128]{1,0:T(8,128)(2,1)S(1)} %get-tuple-element.24), channel_id=1, source_target_pairs={{0,3},{1,2},{2,1},{3,0},{4,7},{5,6},{6,5},{7,4},{8,11},{9,10},{10,... | collective-permute-start | bytes 399368 | tf_op jit(solution)/shard_map/ppermute | solution.py:37

commit v3 on v2

--- a/solution.py
+++ b/solution.py
@@ -176,11 +176,12 @@
     return base + jnp.concatenate(suns, axis=1)
 
 
-def grad_terms(me_ref, base_ref, closed_ref, target_ref, codes, masks, linear, square):
+def grad_terms(me_ref, base_ref, closed_ref, target_ref, codes, crosses, masks, linear, square):
     rows, width = base_ref.shape[0], linear.shape[1]
-    for mask, code in zip(masks, codes):
+    for mask, code, cross_ref in zip(masks, codes, crosses):
         at = place(me_ref, mask, width)
         cross = cross_of(code, base_ref[:, at])
+        cross_ref[:] = cross
         apart = closed_ref[:, at] - target_ref[:, at].astype(jnp.float32)
         linear = linear + jnp.sum((apart * cross).reshape(rows // 8, 8, width), axis=0)
         square = square + jnp.sum((cross * cross).reshape(rows // 8, 8, width), axis=0)
@@ -188,19 +189,25 @@
 
 
 def first_kernel(masks):
+    count = len(masks)
+
     def kernel(me_ref, base_ref, closed_ref, target_ref, *refs):
-        codes, out_ref = refs[:-1], refs[-1]
+        codes, crosses, out_ref = refs[:count], refs[count : 2 * count], refs[-1]
         zero = jnp.zeros(out_ref.shape[1:], jnp.float32)
-        out_ref[0], out_ref[1] = grad_terms(me_ref, base_ref, closed_ref, target_ref, codes, masks, zero, zero)
+        out_ref[0], out_ref[1] = grad_terms(
+            me_ref, base_ref, closed_ref, target_ref, codes, crosses, masks, zero, zero
+        )
 
     return kernel
 
 
 def second_kernel(masks, zones):
+    count = len(masks)
+
     def kernel(me_ref, own_ref, base_ref, closed_ref, target_ref, first_ref, sums_ref, *refs):
-        codes, out_ref = refs[:-1], refs[-1]
+        codes, crosses, out_ref = refs[:count], refs[count : 2 * count], refs[-1]
         linear, square = grad_terms(
-            me_ref, base_ref, closed_ref, target_ref, codes, masks, first_ref[0], first_ref[1]
+            me_ref, base_ref, closed_ref, target_ref, codes, crosses, masks, first_ref[0], first_ref[1]
         )
         lane = lax.broadcasted_iota(jnp.int32, sums_ref.shape, 1)
         row = jnp.where(lane == own_ref[0], 2.0 * jnp.sum(linear, keepdims=True), sums_ref[:])
@@ -211,8 +218,8 @@
 
 
 def last_kernel(groups, zones, windows):
-    def kernel(place_ref, own_ref, heard_ref, zone_ref, area_ref, openness_ref, base_ref, closed_ref, *refs):
-        codes, (lit_ref, step_ref) = refs[:groups], refs[groups:]
+    def kernel(place_ref, own_ref, heard_ref, zone_ref, area_ref, openness_ref, closed_ref, *refs):
+        crosses, (lit_ref, step_ref) = refs[:groups], refs[groups:]
         total = jnp.sum(heard_ref[:], axis=0)
         linear, quadratic, num, den, squares = [total[:, i * zones : (i + 1) * zones] for i in range(5)]
         share = num / den
@@ -221,7 +228,7 @@
         width = closed_ref.shape[1] // groups
         for mask in range(groups):
             at = place(place_ref, mask, width)
-            lit = closed_ref[:, at] + own_share * cross_of(codes[mask], base_ref[:, at])
+            lit = closed_ref[:, at] + own_share * crosses[mask][:]
             lit_ref[:, at] = lit.astype(jnp.bfloat16)
         ratio = groups * (linear + share * quadratic) / den
         rms = jnp.sqrt(jnp.sum(ratio * ratio * squares, keepdims=True) / (windows * groups) + 1e-06)
@@ -313,25 +320,29 @@
         ],
     )(codes[0], sky.T, sky_open, sky_closed, target)
     first, second = [2, 0], [1, 3]
-    first_sums = call(
+    block = shape((rows, width), f32)
+    *first_crosses, first_sums = call(
         first_kernel(first),
         "first",
-        shape((2, 8, width), f32),
+        [block] * len(first) + [shape((2, 8, width), f32)],
         in_specs=[SMEM] + [VMEM] * (3 + len(first)),
+        out_specs=[VMEM] * (1 + len(first)),
     )(me, base, closed, wanted, *[codes[mask] for mask in first])
-    sent = call(
+    *second_crosses, sent = call(
         second_kernel(second, zones),
         "second",
-        shape((zones * groups, 1, message), f32),
+        [block] * len(second) + [shape((zones * groups, 1, message), f32)],
         in_specs=[SMEM] * 2 + [VMEM] * (5 + len(second)),
+        out_specs=[VMEM] * (1 + len(second)),
     )(me, own_zone, base, closed, wanted, first_sums, zone_sums, *[codes[mask] for mask in second])
-    heard = lax.all_to_all(sent, ("sens", "hour"), 0, 0)
+    crosses = dict(zip(first + second, first_crosses + second_crosses))
+    heard = lax.all_to_all(sent, ("hour", "sens"), 0, 0)
     illuminance, new_openness = call(
         last_kernel(groups, zones, windows * zones),
         "last",
         [shape((rows, sensors), bf16), shape(tiles, f32)],
-        in_specs=[SMEM] * 2 + [VMEM] * (6 + groups),
-    )(me, own_zone, heard, zone2, area2, openness2, base, closed, *codes)
+        in_specs=[SMEM] * 2 + [VMEM] * (5 + groups),
+    )(me, own_zone, heard, zone2, area2, openness2, closed, *[crosses[mask] for mask in range(groups)])
     return (illuminance, new_openness.reshape(-1))
 
 

time: 37.1 us -> 36.9 us (level)
  no operation moved by 1% of the time
where the time goes in v3:
time: 36.9 us; the launch traced here: 36.7 us
  Pallas kernels  11.8 us (32%)
  blocking collectives  10.4 us (28%)
  starting transfers between devices  10.3 us (28%)
  waiting for transfers between devices  3.44 us (9%)
  between operations  0.71 us (2%)
    pallas_call x10, Pallas kernels, call(): run(*[pltpu.with_memory_space_constraint(x, pltpu.HBM) if s is HBM else x...  11.8 us
    all_to_all x1, blocking collectives, local(): heard = lax.all_to_all(sent, ('hour', 'sens'), 0, 0)  10.4 us
    ppermute x5, starting transfers between devices, exchange(): lax.ppermute(x, axis, [(i, i ^ mask) for i in range(lax.axis_size(axis))])  10.3 us
    ppermute x5, waiting for transfers between devices, exchange(): lax.ppermute(x, axis, [(i, i ^ mask) for i in range(lax.axis_size(axis))])  3.44 us
  transfers between devices with their start and end apart: 5, of which 2 were waited for; matrix products, arithmetic and copies ran while one was open for 0% of the time, Pallas kernels for 26%

profile of v3, /device:TPU:0, one launch (start us, length us, event | category | flops | bytes accessed | tf_op | source)
XLA Modules:
  0.0 36.7 jit_solution(18059886770985054573)
XLA Ops:
  0.6 0.7 %pack.1.refs_0_.one_ref = bf16[16,128]{1,0:T(8,128)(2,1)S(1)} custom-call(s32[1]{0:T(128)} %bitcast.me_ref.place_ref, s32[1]{0:T(128)} %bitcast.1.own_ref, s32[4,128]{1,0:T(4,128)} %bitcast.13, bf16[4,128]{1,0:T(4,128)(2,1)} %bitcast.14), custom_call_target="tpu_custom_call" | custom-call | tf_op jit(solution)/shard_map/pack/pallas_call | solution.py:31
  1.4 4.1 %collective-permute-start = (bf16[16,128]{1,0:T(8,128)(2,1)S(1)}, bf16[16,128]{1,0:T(8,128)(2,1)S(1)}, u32[]{:S(2)}, u32[]{:S(2)}) collective-permute-start(bf16[16,128]{1,0:T(8,128)(2,1)S(1)} %pack.1.refs_0_.one_ref), channel_id=1, source_target_pairs={{0,2},{1,3},{2,0},{3,1},{4,6},{5,7},{6,4},{7,5},{8,10},{9,11},{10,... | collective-permute-start | bytes 12296 | tf_op jit(solution)/shard_map/ppermute | solution.py:37
  5.5 2.3 %fetch.1 = (bf16[4096,512]{1,0:T(8,128)(2,1)S(1)}, f32[1,128]{1,0:T(1,128)S(1)}, s32[8,128]{1,0:T(8,128)S(1)}, f32[8,128]{1,0:T(8,128)S(1)}, f32[8,128]{1,0:T(8,128)S(1)}) custom-call(bf16[5165,512]{1,0:T(8,128)(2,1)} %rest_in.1, s32[8,128]{1,0:T(8,128)} %bitcast.10, f32[8,128]{1,0:T(8,128)} %bitcast.11, f32[8,128]{1,0:T(8,128)} %bitcast.12), custom_call_target="tpu_custom_call" | custom-call | tf_op jit(solution)/shard_map/fetch/pallas_call | solution.py:31
  7.7 0.0 collective-permute-done.refs_0_.two_ref
  7.8 1.6 %collective-permute-start.2 = (bf16[32,128]{1,0:T(8,128)(2,1)S(1)}, bf16[32,128]{1,0:T(8,128)(2,1)S(1)}, u32[]{:S(2)}, u32[]{:S(2)}) collective-permute-start(bf16[32,128]{1,0:T(8,128)(2,1)S(1)} %join.1), channel_id=1, source_target_pairs={{0,1},{1,0},{2,3},{3,2},{4,5},{5,4},{6,7},{7,6},{8,9},{9,8},{10,11... | collective-permute-start | bytes 24584 | tf_op jit(solution)/shard_map/ppermute | solution.py:37
  9.4 1.7 %sun.3 = (s16[520,128]{1,0:T(8,128)(2,1)S(1)}, bf16[1069,512]{1,0:T(8,128)(2,1)S(1)}) custom-call(bf16[4096,512]{1,0:T(8,128)(2,1)S(1)} %get-tuple-element.22.first_ref, bf16[5165,512]{1,0:T(8,128)(2,1)} %rest_in.1, bf16[16,128]{1,0:T(8,128)(2,1)S(1)} %collective-permute-done.refs_0_.two_ref), custom_call_target="tpu_custom_call" | custom-call | tf_op jit(solution)/shard_map/sun/pallas_call | solution.py:31
  11.1 2.2 %collective-permute-start.1 = (s16[520,128]{1,0:T(8,128)(2,1)S(1)}, s16[520,128]{1,0:T(8,128)(2,1)S(1)}, u32[]{:S(2)}, u32[]{:S(2)}) collective-permute-start(s16[520,128]{1,0:T(8,128)(2,1)S(1)} %get-tuple-element.27), channel_id=1, source_target_pairs={{0,2},{1,3},{2,0},{3,1},{4,6},{5,7},{6,4},{7,5},{8,10},{9,11},{10,... | collective-permute-start | bytes 399368 | tf_op jit(solution)/shard_map/ppermute | solution.py:37
  13.3 0.0 collective-permute-done.2.refs_0_
  13.3 2.2 %sun.5 = (s16[520,128]{1,0:T(8,128)(2,1)S(1)}, s16[520,128]{1,0:T(8,128)(2,1)S(1)}) custom-call(bf16[4096,512]{1,0:T(8,128)(2,1)S(1)} %get-tuple-element.22.first_ref, bf16[1069,512]{1,0:T(8,128)(2,1)S(1)} %get-tuple-element.23.rest_in, bf16[32,128]{1,0:T(8,128)(2,1)S(1)} %collective-permute-done.2.refs_0_), custom_call_target="tpu_custom_call" | custom-call | tf_op jit(solution)/shard_map/sun/pallas_call | solution.py:31
  15.5 0.5 %collective-permute-start.3 = (s16[520,128]{1,0:T(8,128)(2,1)S(1)}, s16[520,128]{1,0:T(8,128)(2,1)S(1)}, u32[]{:S(2)}, u32[]{:S(2)}) collective-permute-start(s16[520,128]{1,0:T(8,128)(2,1)S(1)} %get-tuple-element.30), channel_id=1, source_target_pairs={{0,1},{1,0},{2,3},{3,2},{4,5},{5,4},{6,7},{7,6},{8,9},{9,8},{10,11... | collective-permute-start | bytes 399368 | tf_op jit(solution)/shard_map/ppermute | solution.py:37
  16.1 1.8 %collective-permute-start.4 = (s16[520,128]{1,0:T(8,128)(2,1)S(1)}, s16[520,128]{1,0:T(8,128)(2,1)S(1)}, u32[]{:S(2)}, u32[]{:S(2)}) collective-permute-start(s16[520,128]{1,0:T(8,128)(2,1)S(1)} %get-tuple-element.31), channel_id=1, source_target_pairs={{0,3},{1,2},{2,1},{3,0},{4,7},{5,6},{6,5},{7,4},{8,11},{9,10},{10,... | collective-permute-start | bytes 399368 | tf_op jit(solution)/shard_map/ppermute | solution.py:37
  17.9 1.3 %sun.4.token.refs_1_ = s16[520,128]{1,0:T(8,128)(2,1)S(1)} custom-call(bf16[4096,512]{1,0:T(8,128)(2,1)S(1)} %get-tuple-element.22.first_ref, bf16[1069,512]{1,0:T(8,128)(2,1)S(1)} %get-tuple-element.23.rest_in, bf16[16,128]{1,0:T(8,128)(2,1)S(1)} %pack.1.refs_0_.one_ref), custom_call_target="tpu_custom_call" | custom-call | tf_op jit(solution)/shard_map/sun/pallas_call | solution.py:31
  19.2 1.8 %base.1 = (f32[128,2048]{1,0:T(8,128)S(1)}, f32[128,2048]{1,0:T(8,128)S(1)}, bf16[128,2048]{1,0:T(8,128)(2,1)S(1)}) custom-call(s16[520,128]{1,0:T(8,128)(2,1)S(1)} %sun.4.token.refs_1_, bf16[146,128]{1,0:T(8,128)(2,1)} %bitcast.9, bf16[146,2048]{1,0:T(8,128)(2,1)} %open_hbm.1, bf16[146,2048]{1,0:T(8,128)(2,1)} %closed_hbm.1, bf16[128,2048]{1,0:T(8,128)(2,1)} %target_hbm.1), custom_call_target="tpu_custom_call" | custom-call | tf_op jit(solution)/shard_map/base/pallas_call | solution.py:31
  21.0 0.3 collective-permute-done.1.refs_0_
  21.3 0.2 first.1
  21.5 3.1 %collective-permute-done.3.refs_0_ = s16[520,128]{1,0:T(8,128)(2,1)S(1)} collective-permute-done((s16[520,128]{1,0:T(8,128)(2,1)S(1)}, s16[520,128]{1,0:T(8,128)(2,1)S(1)}, u32[]{:S(2)}, u32[]{:S(2)}) %collective-permute-start.3) | collective-permute-done | bytes 133152 | tf_op jit(solution)/shard_map/ppermute | solution.py:37
  24.6 0.0 collective-permute-done.4.refs_1_
  24.6 0.4 %second.1 = (f32[128,512]{1,0:T(8,128)S(1)}, f32[128,512]{1,0:T(8,128)S(1)}, f32[32,1,128]{2,1,0:T(1,128)S(1)}) custom-call(s32[1]{0:T(128)} %bitcast.me_ref.place_ref, s32[1]{0:T(128)} %bitcast.1.own_ref, f32[128,2048]{1,0:T(8,128)S(1)} %get-tuple-element.24.base_ref, f32[128,2048]{1,0:T(8,128)S(1)} %get-tuple-element.25.closed_ref, ...), custom_call_target="tpu_custom_call" | custom-call | tf_op jit(solution)/shard_map/second/pallas_call | solution.py:31
  25.0 10.4 %all_to_all.5.heard_ref = f32[32,1,128]{2,1,0:T(1,128)S(1)} all-to-all(f32[32,1,128]{2,1,0:T(1,128)S(1)} %get-tuple-element.32), channel_id=1, replica_groups=mesh['sens'=8,'hour'=4] {'hour','sens'}, dimensions={0} | all-to-all | bytes 32768 | tf_op jit(solution)/shard_map/all_to_all | solution.py:339
  35.4 1.3 %last.1 = (bf16[128,2048]{1,0:T(8,128)(2,1)}, f32[8,128]{1,0:T(8,128)}) custom-call(s32[1]{0:T(128)} %bitcast.me_ref.place_ref, s32[1]{0:T(128)} %bitcast.1.own_ref, f32[32,1,128]{2,1,0:T(1,128)S(1)} %all_to_all.5.heard_ref, s32[8,128]{1,0:T(8,128)S(1)} %get-tuple-element.33.zone_ref, f32[8,128]{1,0:T(8,128)S(1)} %get-tuple-element.34.area_ref, ...), custom_call_target="tpu_custom_call" | custom-call | tf_op jit(solution)/shard_map/last/pallas_call | solution.py:31
  (1 shorter events, 0.0 us)
Async XLA Ops:
  1.4 6.4 %collective-permute-start = (bf16[16,128]{1,0:T(8,128)(2,1)S(1)}, bf16[16,128]{1,0:T(8,128)(2,1)S(1)}, u32[]{:S(2)}, u32[]{:S(2)}) collective-permute-start(bf16[16,128]{1,0:T(8,128)(2,1)S(1)} %pack.1.refs_0_.one_ref), channel_id=1, source_target_pairs={{0,2},{1,3},{2,0},{3,1},{4,6},{5,7},{6,4},{7,5},{8,10},{9,11},{10,... | collective-permute-start | bytes 12296 | tf_op jit(solution)/shard_map/ppermute | solution.py:37
  7.8 5.5 %collective-permute-start.2 = (bf16[32,128]{1,0:T(8,128)(2,1)S(1)}, bf16[32,128]{1,0:T(8,128)(2,1)S(1)}, u32[]{:S(2)}, u32[]{:S(2)}) collective-permute-start(bf16[32,128]{1,0:T(8,128)(2,1)S(1)} %join.1), channel_id=1, source_target_pairs={{0,1},{1,0},{2,3},{3,2},{4,5},{5,4},{6,7},{7,6},{8,9},{9,8},{10,11... | collective-permute-start | bytes 24584 | tf_op jit(solution)/shard_map/ppermute | solution.py:37
  11.1 10.2 %collective-permute-start.1 = (s16[520,128]{1,0:T(8,128)(2,1)S(1)}, s16[520,128]{1,0:T(8,128)(2,1)S(1)}, u32[]{:S(2)}, u32[]{:S(2)}) collective-permute-start(s16[520,128]{1,0:T(8,128)(2,1)S(1)} %get-tuple-element.27), channel_id=1, source_target_pairs={{0,2},{1,3},{2,0},{3,1},{4,6},{5,7},{6,4},{7,5},{8,10},{9,11},{10,... | collective-permute-start | bytes 399368 | tf_op jit(solution)/shard_map/ppermute | solution.py:37
  15.5 9.1 %collective-permute-start.3 = (s16[520,128]{1,0:T(8,128)(2,1)S(1)}, s16[520,128]{1,0:T(8,128)(2,1)S(1)}, u32[]{:S(2)}, u32[]{:S(2)}) collective-permute-start(s16[520,128]{1,0:T(8,128)(2,1)S(1)} %get-tuple-element.30), channel_id=1, source_target_pairs={{0,1},{1,0},{2,3},{3,2},{4,5},{5,4},{6,7},{7,6},{8,9},{9,8},{10,11... | collective-permute-start | bytes 399368 | tf_op jit(solution)/shard_map/ppermute | solution.py:37
  16.1 8.6 %collective-permute-start.4 = (s16[520,128]{1,0:T(8,128)(2,1)S(1)}, s16[520,128]{1,0:T(8,128)(2,1)S(1)}, u32[]{:S(2)}, u32[]{:S(2)}) collective-permute-start(s16[520,128]{1,0:T(8,128)(2,1)S(1)} %get-tuple-element.31), channel_id=1, source_target_pairs={{0,3},{1,2},{2,1},{3,0},{4,7},{5,6},{6,5},{7,4},{8,11},{9,10},{10,... | collective-permute-start | bytes 399368 | tf_op jit(solution)/shard_map/ppermute | solution.py:37

commit v4 on v3

--- a/solution.py
+++ b/solution.py
@@ -57,7 +57,7 @@
 def fetch_kernel(zones):
     def kernel(coef_hbm, zone_hbm, area_hbm, openness_hbm, coef_ref, sums_ref, zone_ref, area_ref, openness_ref, sems):
         pairs = [(zone_hbm, zone_ref), (area_hbm, area_ref), (openness_hbm, openness_ref)]
-        copies = fetch(pairs + [(coef_hbm.at[pl.ds(0, coef_ref.shape[0])], coef_ref)], sems)
+        copies = fetch(pairs + [(coef_hbm, coef_ref)], sems)
         for c in copies[:3]:
             c.wait()
         zone, area = zone_ref[:], area_ref[:]
@@ -80,32 +80,16 @@
     out_ref[HEAD:] = two_ref[:]
 
 
-def sun_kernel(sources, kbins, stream):
+def sun_kernel(sources, kbins):
     count = len(sources)
     inputs = 1 + max(operand for operand, _ in sources)
 
-    def kernel(first_ref, rest_in, *refs):
-        heads, outs, rest = refs[:inputs], refs[inputs : inputs + count], refs[inputs + count :]
+    def kernel(coef_ref, *refs):
+        heads, outs, (acc, pattern, block) = refs[:inputs], refs[inputs : inputs + count], refs[inputs + count :]
         rows = heads[0].shape[1]
-        split = first_ref.shape[0]
-        nbins = split + rest_in.shape[0] - (split if stream else 0)
+        nbins = coef_ref.shape[0]
         step = CHUNK * LANES
         spans = [(first, min(first + step, nbins)) for first in range(0, nbins, step)]
-        if stream:
-            rest_ref, acc, pattern, block, sems = rest
-            late = [span for span in spans if span[0] >= split]
-            cuts = late[:-2] + [(late[-2][0], nbins)]
-            copies = fetch(
-                [
-                    (rest_in.at[pl.ds(first, end - first)], rest_ref.at[pl.ds(first - split, end - first)])
-                    for first, end in cuts
-                ],
-                sems,
-            )
-            waits = {first: c for (first, _), c in zip(cuts, copies)}
-        else:
-            rest_ref, (acc, pattern, block) = rest_in, rest
-            waits = {}
         lane = lax.broadcasted_iota(jnp.int32, (rows, LANES), 1)
         for g in range(count):
             operand, offset = sources[g]
@@ -126,10 +110,7 @@
                 here = block[:] == jnp.asarray(c, block.dtype)
                 parts.append(jnp.where(here, pattern[:], jnp.zeros_like(pattern)).astype(jnp.bfloat16))
             weights = jnp.concatenate(parts, axis=1) if len(parts) > 1 else parts[0]
-            if first in waits:
-                waits[first].wait()
-            coef = first_ref[first:end] if first < split else rest_ref[first - split : end - split]
-            part = jnp.dot(weights[:, : end - first], coef, preferred_element_type=jnp.float32)
+            part = jnp.dot(weights[:, : end - first], coef_ref[first:end], preferred_element_type=jnp.float32)
             acc[:] = part if first == 0 else acc[:] + part
 
         for g in range(count):
@@ -270,12 +251,10 @@
 
     tiles = (windows // LANES, LANES)
     message = pl.cdiv(5 * zones, LANES) * LANES
-    split = (nbins // (CHUNK * LANES) - 1) * CHUNK * LANES
-    assert 0 < split and split + CHUNK * LANES < nbins
     coef, zone_sums, zone2, area2, openness2 = call(
         fetch_kernel(zones),
         "fetch",
-        [shape((split, width), bf16), shape((1, message), f32)]
+        [shape((nbins, width), bf16), shape((1, message), f32)]
         + [shape(tiles, jnp.int32), shape(tiles, f32), shape(tiles, f32)],
         in_specs=[HBM] * 4,
         out_specs=[VMEM] * 5,
@@ -287,23 +266,22 @@
 
     assert width // LANES <= TAIL
 
-    def sun(sources, rest, stream, *heads):
+    def sun(sources, *heads):
         count = len(sources)
-        late = [shape((nbins - split, width), bf16)] if stream else []
         scratch = [pltpu.VMEM((count * rows, width), f32)] + [pltpu.VMEM((count * rows, LANES), PATTERN)] * 2
         return call(
-            sun_kernel(sources, kbins, stream),
+            sun_kernel(sources, kbins),
             "sun",
-            [shape((width // LANES * rows + TAIL, LANES), jnp.int16)] * count + late,
-            in_specs=[VMEM, HBM if stream else VMEM] + [VMEM] * len(heads),
-            out_specs=[VMEM] * (count + len(late)),
-            scratch_shapes=scratch + ([dma(1)] if stream else []),
-        )(coef, rest, *heads)
+            [shape((width // LANES * rows + TAIL, LANES), jnp.int16)] * count,
+            in_specs=[VMEM] * (1 + len(heads)),
+            out_specs=[VMEM] * count,
+            scratch_shapes=scratch,
+        )(coef, *heads)
 
     codes = [None] * groups
-    codes[2], late = sun([(0, 0)], sun_coef, True, far)
-    codes[1], codes[3] = sun([(0, 0), (0, HEAD)], late, False, near)
-    (codes[0],) = sun([(0, 0)], late, False, packed)
+    (codes[2],) = sun([(0, 0)], far)
+    codes[1], codes[3] = sun([(0, 0), (0, HEAD)], near)
+    (codes[0],) = sun([(0, 0)], packed)
     codes = [exchange(code, "hour", mask) if mask else code for mask, code in enumerate(codes)]
 
     base, closed, wanted = call(

time: 36.9 us -> 36.9 us (level)
  no operation moved by 1% of the time
where the time goes in v4:
time: 36.9 us; the launch traced here: 36.6 us
  Pallas kernels  11.8 us (32%)
  blocking collectives  10.7 us (29%)
  starting transfers between devices  10.3 us (28%)
  waiting for transfers between devices  3.14 us (9%)
  between operations  0.71 us (2%)
    pallas_call x10, Pallas kernels, call(): run(*[pltpu.with_memory_space_constraint(x, pltpu.HBM) if s is HBM else x...  11.8 us
    all_to_all x1, blocking collectives, local(): heard = lax.all_to_all(sent, ('hour', 'sens'), 0, 0)  10.7 us
    ppermute x5, starting transfers between devices, exchange(): lax.ppermute(x, axis, [(i, i ^ mask) for i in range(lax.axis_size(axis))])  10.3 us
    ppermute x5, waiting for transfers between devices, exchange(): lax.ppermute(x, axis, [(i, i ^ mask) for i in range(lax.axis_size(axis))])  3.14 us
  transfers between devices with their start and end apart: 5, of which 2 were waited for; matrix products, arithmetic and copies ran while one was open for 0% of the time, Pallas kernels for 26%

profile of v4, /device:TPU:0, one launch (start us, length us, event | category | flops | bytes accessed | tf_op | source)
XLA Modules:
  0.0 36.6 jit_solution(18363704136551068823)
XLA Ops:
  0.6 0.7 %pack.1.refs_0_.one_ref = bf16[16,128]{1,0:T(8,128)(2,1)S(1)} custom-call(s32[1]{0:T(128)} %bitcast.me_ref.place_ref, s32[1]{0:T(128)} %bitcast.1.own_ref, s32[4,128]{1,0:T(4,128)} %bitcast.13, bf16[4,128]{1,0:T(4,128)(2,1)} %bitcast.14), custom_call_target="tpu_custom_call" | custom-call | tf_op jit(solution)/shard_map/pack/pallas_call | solution.py:31
  1.4 4.1 %collective-permute-start = (bf16[16,128]{1,0:T(8,128)(2,1)S(1)}, bf16[16,128]{1,0:T(8,128)(2,1)S(1)}, u32[]{:S(2)}, u32[]{:S(2)}) collective-permute-start(bf16[16,128]{1,0:T(8,128)(2,1)S(1)} %pack.1.refs_0_.one_ref), channel_id=1, source_target_pairs={{0,2},{1,3},{2,0},{3,1},{4,6},{5,7},{6,4},{7,5},{8,10},{9,11},{10,... | collective-permute-start | bytes 12296 | tf_op jit(solution)/shard_map/ppermute | solution.py:37
  5.5 2.6 %fetch.1 = (bf16[5165,512]{1,0:T(8,128)(2,1)S(1)}, f32[1,128]{1,0:T(1,128)S(1)}, s32[8,128]{1,0:T(8,128)S(1)}, f32[8,128]{1,0:T(8,128)S(1)}, f32[8,128]{1,0:T(8,128)S(1)}) custom-call(bf16[5165,512]{1,0:T(8,128)(2,1)} %coef_hbm.1, s32[8,128]{1,0:T(8,128)} %bitcast.10, f32[8,128]{1,0:T(8,128)} %bitcast.11, f32[8,128]{1,0:T(8,128)} %bitcast.12), custom_call_target="tpu_custom_call" | custom-call | tf_op jit(solution)/shard_map/fetch/pallas_call | solution.py:31
  8.1 0.0 collective-permute-done.refs_0_.two_ref
  8.1 1.6 %collective-permute-start.2 = (bf16[32,128]{1,0:T(8,128)(2,1)S(1)}, bf16[32,128]{1,0:T(8,128)(2,1)S(1)}, u32[]{:S(2)}, u32[]{:S(2)}) collective-permute-start(bf16[32,128]{1,0:T(8,128)(2,1)S(1)} %join.1), channel_id=1, source_target_pairs={{0,1},{1,0},{2,3},{3,2},{4,5},{5,4},{6,7},{7,6},{8,9},{9,8},{10,11... | collective-permute-start | bytes 24584 | tf_op jit(solution)/shard_map/ppermute | solution.py:37
  9.7 1.3 %sun.4 = s16[520,128]{1,0:T(8,128)(2,1)S(1)} custom-call(bf16[5165,512]{1,0:T(8,128)(2,1)S(1)} %get-tuple-element.20.coef_ref, bf16[16,128]{1,0:T(8,128)(2,1)S(1)} %collective-permute-done.refs_0_.two_ref), custom_call_target="tpu_custom_call" | custom-call | tf_op jit(solution)/shard_map/sun/pallas_call | solution.py:31
  11.0 1.9 %collective-permute-start.1 = (s16[520,128]{1,0:T(8,128)(2,1)S(1)}, s16[520,128]{1,0:T(8,128)(2,1)S(1)}, u32[]{:S(2)}, u32[]{:S(2)}) collective-permute-start(s16[520,128]{1,0:T(8,128)(2,1)S(1)} %sun.4), channel_id=1, source_target_pairs={{0,2},{1,3},{2,0},{3,1},{4,6},{5,7},{6,4},{7,5},{8,10},{9,11},{10,... | collective-permute-start | bytes 399368 | tf_op jit(solution)/shard_map/ppermute | solution.py:37
  12.9 0.0 collective-permute-done.2.refs_0_
  12.9 2.2 %sun.5 = (s16[520,128]{1,0:T(8,128)(2,1)S(1)}, s16[520,128]{1,0:T(8,128)(2,1)S(1)}) custom-call(bf16[5165,512]{1,0:T(8,128)(2,1)S(1)} %get-tuple-element.20.coef_ref, bf16[32,128]{1,0:T(8,128)(2,1)S(1)} %collective-permute-done.2.refs_0_), custom_call_target="tpu_custom_call" | custom-call | tf_op jit(solution)/shard_map/sun/pallas_call | solution.py:31
  15.2 0.5 %collective-permute-start.3 = (s16[520,128]{1,0:T(8,128)(2,1)S(1)}, s16[520,128]{1,0:T(8,128)(2,1)S(1)}, u32[]{:S(2)}, u32[]{:S(2)}) collective-permute-start(s16[520,128]{1,0:T(8,128)(2,1)S(1)} %get-tuple-element.26), channel_id=1, source_target_pairs={{0,1},{1,0},{2,3},{3,2},{4,5},{5,4},{6,7},{7,6},{8,9},{9,8},{10,11... | collective-permute-start | bytes 399368 | tf_op jit(solution)/shard_map/ppermute | solution.py:37
  15.7 2.1 %collective-permute-start.4 = (s16[520,128]{1,0:T(8,128)(2,1)S(1)}, s16[520,128]{1,0:T(8,128)(2,1)S(1)}, u32[]{:S(2)}, u32[]{:S(2)}) collective-permute-start(s16[520,128]{1,0:T(8,128)(2,1)S(1)} %get-tuple-element.27), channel_id=1, source_target_pairs={{0,3},{1,2},{2,1},{3,0},{4,7},{5,6},{6,5},{7,4},{8,11},{9,10},{10,... | collective-permute-start | bytes 399368 | tf_op jit(solution)/shard_map/ppermute | solution.py:37
  17.8 1.3 %sun.3.token.refs_1_ = s16[520,128]{1,0:T(8,128)(2,1)S(1)} custom-call(bf16[5165,512]{1,0:T(8,128)(2,1)S(1)} %get-tuple-element.20.coef_ref, bf16[16,128]{1,0:T(8,128)(2,1)S(1)} %pack.1.refs_0_.one_ref), custom_call_target="tpu_custom_call" | custom-call | tf_op jit(solution)/shard_map/sun/pallas_call | solution.py:31
  19.1 1.8 %base.1 = (f32[128,2048]{1,0:T(8,128)S(1)}, f32[128,2048]{1,0:T(8,128)S(1)}, bf16[128,2048]{1,0:T(8,128)(2,1)S(1)}) custom-call(s16[520,128]{1,0:T(8,128)(2,1)S(1)} %sun.3.token.refs_1_, bf16[146,128]{1,0:T(8,128)(2,1)} %bitcast.9, bf16[146,2048]{1,0:T(8,128)(2,1)} %open_hbm.1, bf16[146,2048]{1,0:T(8,128)(2,1)} %closed_hbm.1, bf16[128,2048]{1,0:T(8,128)(2,1)} %target_hbm.1), custom_call_target="tpu_custom_call" | custom-call | tf_op jit(solution)/shard_map/base/pallas_call | solution.py:31
  20.9 0.3 collective-permute-done.1.refs_0_
  21.2 0.2 first.1
  21.4 2.8 %collective-permute-done.3.refs_0_ = s16[520,128]{1,0:T(8,128)(2,1)S(1)} collective-permute-done((s16[520,128]{1,0:T(8,128)(2,1)S(1)}, s16[520,128]{1,0:T(8,128)(2,1)S(1)}, u32[]{:S(2)}, u32[]{:S(2)}) %collective-permute-start.3) | collective-permute-done | bytes 133152 | tf_op jit(solution)/shard_map/ppermute | solution.py:37
  24.3 0.0 collective-permute-done.4.refs_1_
  24.3 0.4 %second.1 = (f32[128,512]{1,0:T(8,128)S(1)}, f32[128,512]{1,0:T(8,128)S(1)}, f32[32,1,128]{2,1,0:T(1,128)S(1)}) custom-call(s32[1]{0:T(128)} %bitcast.me_ref.place_ref, s32[1]{0:T(128)} %bitcast.1.own_ref, f32[128,2048]{1,0:T(8,128)S(1)} %get-tuple-element.21.base_ref, f32[128,2048]{1,0:T(8,128)S(1)} %get-tuple-element.22.closed_ref, ...), custom_call_target="tpu_custom_call" | custom-call | tf_op jit(solution)/shard_map/second/pallas_call | solution.py:31
  24.6 10.7 %all_to_all.5.heard_ref = f32[32,1,128]{2,1,0:T(1,128)S(1)} all-to-all(f32[32,1,128]{2,1,0:T(1,128)S(1)} %get-tuple-element.28), channel_id=1, replica_groups=mesh['sens'=8,'hour'=4] {'hour','sens'}, dimensions={0} | all-to-all | bytes 32768 | tf_op jit(solution)/shard_map/all_to_all | solution.py:317
  35.4 1.3 %last.1 = (bf16[128,2048]{1,0:T(8,128)(2,1)}, f32[8,128]{1,0:T(8,128)}) custom-call(s32[1]{0:T(128)} %bitcast.me_ref.place_ref, s32[1]{0:T(128)} %bitcast.1.own_ref, f32[32,1,128]{2,1,0:T(1,128)S(1)} %all_to_all.5.heard_ref, s32[8,128]{1,0:T(8,128)S(1)} %get-tuple-element.29.zone_ref, f32[8,128]{1,0:T(8,128)S(1)} %get-tuple-element.30.area_ref, ...), custom_call_target="tpu_custom_call" | custom-call | tf_op jit(solution)/shard_map/last/pallas_call | solution.py:31
  (1 shorter events, 0.0 us)
Async XLA Ops:
  1.4 6.7 %collective-permute-start = (bf16[16,128]{1,0:T(8,128)(2,1)S(1)}, bf16[16,128]{1,0:T(8,128)(2,1)S(1)}, u32[]{:S(2)}, u32[]{:S(2)}) collective-permute-start(bf16[16,128]{1,0:T(8,128)(2,1)S(1)} %pack.1.refs_0_.one_ref), channel_id=1, source_target_pairs={{0,2},{1,3},{2,0},{3,1},{4,6},{5,7},{6,4},{7,5},{8,10},{9,11},{10,... | collective-permute-start | bytes 12296 | tf_op jit(solution)/shard_map/ppermute | solution.py:37
  8.1 4.9 %collective-permute-start.2 = (bf16[32,128]{1,0:T(8,128)(2,1)S(1)}, bf16[32,128]{1,0:T(8,128)(2,1)S(1)}, u32[]{:S(2)}, u32[]{:S(2)}) collective-permute-start(bf16[32,128]{1,0:T(8,128)(2,1)S(1)} %join.1), channel_id=1, source_target_pairs={{0,1},{1,0},{2,3},{3,2},{4,5},{5,4},{6,7},{7,6},{8,9},{9,8},{10,11... | collective-permute-start | bytes 24584 | tf_op jit(solution)/shard_map/ppermute | solution.py:37
  11.0 10.2 %collective-permute-start.1 = (s16[520,128]{1,0:T(8,128)(2,1)S(1)}, s16[520,128]{1,0:T(8,128)(2,1)S(1)}, u32[]{:S(2)}, u32[]{:S(2)}) collective-permute-start(s16[520,128]{1,0:T(8,128)(2,1)S(1)} %sun.4), channel_id=1, source_target_pairs={{0,2},{1,3},{2,0},{3,1},{4,6},{5,7},{6,4},{7,5},{8,10},{9,11},{10,... | collective-permute-start | bytes 399368 | tf_op jit(solution)/shard_map/ppermute | solution.py:37
  15.2 9.1 %collective-permute-start.3 = (s16[520,128]{1,0:T(8,128)(2,1)S(1)}, s16[520,128]{1,0:T(8,128)(2,1)S(1)}, u32[]{:S(2)}, u32[]{:S(2)}) collective-permute-start(s16[520,128]{1,0:T(8,128)(2,1)S(1)} %get-tuple-element.26), channel_id=1, source_target_pairs={{0,1},{1,0},{2,3},{3,2},{4,5},{5,4},{6,7},{7,6},{8,9},{9,8},{10,11... | collective-permute-start | bytes 399368 | tf_op jit(solution)/shard_map/ppermute | solution.py:37
  15.7 8.6 %collective-permute-start.4 = (s16[520,128]{1,0:T(8,128)(2,1)S(1)}, s16[520,128]{1,0:T(8,128)(2,1)S(1)}, u32[]{:S(2)}, u32[]{:S(2)}) collective-permute-start(s16[520,128]{1,0:T(8,128)(2,1)S(1)} %get-tuple-element.27), channel_id=1, source_target_pairs={{0,3},{1,2},{2,1},{3,0},{4,7},{5,6},{6,5},{7,4},{8,11},{9,10},{10,... | collective-permute-start | bytes 399368 | tf_op jit(solution)/shard_map/ppermute | solution.py:37

commit v5 on v4

--- a/solution.py
+++ b/solution.py
@@ -6,7 +6,7 @@
 from jax.sharding import PartitionSpec as P
 
 LANES = 128
-CHUNK = 8
+CHUNK = 16
 HEAD = 16
 TAIL = 8
 PATTERN = jnp.bfloat16
@@ -297,7 +297,7 @@
             dma(4),
         ],
     )(codes[0], sky.T, sky_open, sky_closed, target)
-    first, second = [2, 0], [1, 3]
+    first, second = [2, 0], [3, 1]
     block = shape((rows, width), f32)
     *first_crosses, first_sums = call(
         first_kernel(first),

time: 36.9 us -> 36.9 us (level)
  waiting for transfers between devices: 3.14 us -> 4.89 us
  starting transfers between devices: 10.3 us -> 9.43 us
  blocking collectives: 10.7 us -> 9.87 us
    ppermute x5, waiting for transfers between devices: 3.14 us -> 4.89 us  [exchange(): lax.ppermute(x, axis, [(i, i ^ mask) for i in range(lax.axis_size(axis))])]
    all_to_all x1, blocking collectives: 10.7 us -> 9.87 us  [local(): heard = lax.all_to_all(sent, ('hour', 'sens'), 0, 0)]
    ppermute x5, starting transfers between devices: 10.3 us -> 9.43 us  [exchange(): lax.ppermute(x, axis, [(i, i ^ mask) for i in range(lax.axis_size(axis))])]
where the time goes in v5:
time: 36.9 us; the launch traced here: 36.7 us
  Pallas kernels  11.7 us (32%)
  blocking collectives  9.87 us (27%)
  starting transfers between devices  9.43 us (26%)
  waiting for transfers between devices  4.89 us (13%)
  between operations  0.72 us (2%)
    pallas_call x10, Pallas kernels, call(): run(*[pltpu.with_memory_space_constraint(x, pltpu.HBM) if s is HBM else x...  11.7 us
    all_to_all x1, blocking collectives, local(): heard = lax.all_to_all(sent, ('hour', 'sens'), 0, 0)  9.87 us
    ppermute x5, starting transfers between devices, exchange(): lax.ppermute(x, axis, [(i, i ^ mask) for i in range(lax.axis_size(axis))])  9.43 us
    ppermute x5, waiting for transfers between devices, exchange(): lax.ppermute(x, axis, [(i, i ^ mask) for i in range(lax.axis_size(axis))])  4.89 us
  transfers between devices with their start and end apart: 5, of which 2 were waited for; matrix products, arithmetic and copies ran while one was open for 0% of the time, Pallas kernels for 26%

profile of v5, /device:TPU:0, one launch (start us, length us, event | category | flops | bytes accessed | tf_op | source)
XLA Modules:
  0.0 36.7 jit_solution(12002099032185901846)
XLA Ops:
  0.6 0.7 %pack.1.refs_0_.one_ref = bf16[16,128]{1,0:T(8,128)(2,1)S(1)} custom-call(s32[1]{0:T(128)} %bitcast.me_ref.place_ref, s32[1]{0:T(128)} %bitcast.1.own_ref, s32[4,128]{1,0:T(4,128)} %bitcast.13, bf16[4,128]{1,0:T(4,128)(2,1)} %bitcast.14), custom_call_target="tpu_custom_call" | custom-call | tf_op jit(solution)/shard_map/pack/pallas_call | solution.py:31
  1.4 4.1 %collective-permute-start = (bf16[16,128]{1,0:T(8,128)(2,1)S(1)}, bf16[16,128]{1,0:T(8,128)(2,1)S(1)}, u32[]{:S(2)}, u32[]{:S(2)}) collective-permute-start(bf16[16,128]{1,0:T(8,128)(2,1)S(1)} %pack.1.refs_0_.one_ref), channel_id=1, source_target_pairs={{0,2},{1,3},{2,0},{3,1},{4,6},{5,7},{6,4},{7,5},{8,10},{9,11},{10,... | collective-permute-start | bytes 12296 | tf_op jit(solution)/shard_map/ppermute | solution.py:37
  5.5 2.6 %fetch.1 = (bf16[5165,512]{1,0:T(8,128)(2,1)S(1)}, f32[1,128]{1,0:T(1,128)S(1)}, s32[8,128]{1,0:T(8,128)S(1)}, f32[8,128]{1,0:T(8,128)S(1)}, f32[8,128]{1,0:T(8,128)S(1)}) custom-call(bf16[5165,512]{1,0:T(8,128)(2,1)} %coef_hbm.1, s32[8,128]{1,0:T(8,128)} %bitcast.10, f32[8,128]{1,0:T(8,128)} %bitcast.11, f32[8,128]{1,0:T(8,128)} %bitcast.12), custom_call_target="tpu_custom_call" | custom-call | tf_op jit(solution)/shard_map/fetch/pallas_call | solution.py:31
  8.1 0.0 collective-permute-done.refs_0_.two_ref
  8.1 1.6 %collective-permute-start.2 = (bf16[32,128]{1,0:T(8,128)(2,1)S(1)}, bf16[32,128]{1,0:T(8,128)(2,1)S(1)}, u32[]{:S(2)}, u32[]{:S(2)}) collective-permute-start(bf16[32,128]{1,0:T(8,128)(2,1)S(1)} %join.1), channel_id=1, source_target_pairs={{0,1},{1,0},{2,3},{3,2},{4,5},{5,4},{6,7},{7,6},{8,9},{9,8},{10,11... | collective-permute-start | bytes 24584 | tf_op jit(solution)/shard_map/ppermute | solution.py:37
  9.7 1.3 %sun.4 = s16[520,128]{1,0:T(8,128)(2,1)S(1)} custom-call(bf16[5165,512]{1,0:T(8,128)(2,1)S(1)} %get-tuple-element.20.coef_ref, bf16[16,128]{1,0:T(8,128)(2,1)S(1)} %collective-permute-done.refs_0_.two_ref), custom_call_target="tpu_custom_call" | custom-call | tf_op jit(solution)/shard_map/sun/pallas_call | solution.py:31
  11.0 1.9 %collective-permute-start.1 = (s16[520,128]{1,0:T(8,128)(2,1)S(1)}, s16[520,128]{1,0:T(8,128)(2,1)S(1)}, u32[]{:S(2)}, u32[]{:S(2)}) collective-permute-start(s16[520,128]{1,0:T(8,128)(2,1)S(1)} %sun.4), channel_id=1, source_target_pairs={{0,2},{1,3},{2,0},{3,1},{4,6},{5,7},{6,4},{7,5},{8,10},{9,11},{10,... | collective-permute-start | bytes 399368 | tf_op jit(solution)/shard_map/ppermute | solution.py:37
  12.9 0.0 collective-permute-done.2.refs_0_
  12.9 2.2 %sun.5 = (s16[520,128]{1,0:T(8,128)(2,1)S(1)}, s16[520,128]{1,0:T(8,128)(2,1)S(1)}) custom-call(bf16[5165,512]{1,0:T(8,128)(2,1)S(1)} %get-tuple-element.20.coef_ref, bf16[32,128]{1,0:T(8,128)(2,1)S(1)} %collective-permute-done.2.refs_0_), custom_call_target="tpu_custom_call" | custom-call | tf_op jit(solution)/shard_map/sun/pallas_call | solution.py:31
  15.2 1.8 %collective-permute-start.3 = (s16[520,128]{1,0:T(8,128)(2,1)S(1)}, s16[520,128]{1,0:T(8,128)(2,1)S(1)}, u32[]{:S(2)}, u32[]{:S(2)}) collective-permute-start(s16[520,128]{1,0:T(8,128)(2,1)S(1)} %get-tuple-element.26), channel_id=1, source_target_pairs={{0,3},{1,2},{2,1},{3,0},{4,7},{5,6},{6,5},{7,4},{8,11},{9,10},{10,... | collective-permute-start | bytes 399368 | tf_op jit(solution)/shard_map/ppermute | solution.py:37
  17.0 0.0 collective-permute-start.4
  17.0 1.3 %sun.3.token.refs_1_ = s16[520,128]{1,0:T(8,128)(2,1)S(1)} custom-call(bf16[5165,512]{1,0:T(8,128)(2,1)S(1)} %get-tuple-element.20.coef_ref, bf16[16,128]{1,0:T(8,128)(2,1)S(1)} %pack.1.refs_0_.one_ref), custom_call_target="tpu_custom_call" | custom-call | tf_op jit(solution)/shard_map/sun/pallas_call | solution.py:31
  18.3 1.8 %base.1 = (f32[128,2048]{1,0:T(8,128)S(1)}, f32[128,2048]{1,0:T(8,128)S(1)}, bf16[128,2048]{1,0:T(8,128)(2,1)S(1)}) custom-call(s16[520,128]{1,0:T(8,128)(2,1)S(1)} %sun.3.token.refs_1_, bf16[146,128]{1,0:T(8,128)(2,1)} %bitcast.9, bf16[146,2048]{1,0:T(8,128)(2,1)} %open_hbm.1, bf16[146,2048]{1,0:T(8,128)(2,1)} %closed_hbm.1, bf16[128,2048]{1,0:T(8,128)(2,1)} %target_hbm.1), custom_call_target="tpu_custom_call" | custom-call | tf_op jit(solution)/shard_map/base/pallas_call | solution.py:31
  20.0 2.5 %collective-permute-done.1.refs_0_ = s16[520,128]{1,0:T(8,128)(2,1)S(1)} collective-permute-done((s16[520,128]{1,0:T(8,128)(2,1)S(1)}, s16[520,128]{1,0:T(8,128)(2,1)S(1)}, u32[]{:S(2)}, u32[]{:S(2)}) %collective-permute-start.1) | collective-permute-done | bytes 133152 | tf_op jit(solution)/shard_map/ppermute | solution.py:37
  22.6 0.2 first.1
  22.8 0.0 collective-permute-done.3.refs_0_
  22.8 2.3 %collective-permute-done.4.refs_1_ = s16[520,128]{1,0:T(8,128)(2,1)S(1)} collective-permute-done((s16[520,128]{1,0:T(8,128)(2,1)S(1)}, s16[520,128]{1,0:T(8,128)(2,1)S(1)}, u32[]{:S(2)}, u32[]{:S(2)}) %collective-permute-start.4) | collective-permute-done | bytes 133152 | tf_op jit(solution)/shard_map/ppermute | solution.py:37
  25.2 0.4 %second.1 = (f32[128,512]{1,0:T(8,128)S(1)}, f32[128,512]{1,0:T(8,128)S(1)}, f32[32,1,128]{2,1,0:T(1,128)S(1)}) custom-call(s32[1]{0:T(128)} %bitcast.me_ref.place_ref, s32[1]{0:T(128)} %bitcast.1.own_ref, f32[128,2048]{1,0:T(8,128)S(1)} %get-tuple-element.21.base_ref, f32[128,2048]{1,0:T(8,128)S(1)} %get-tuple-element.22.closed_ref, ...), custom_call_target="tpu_custom_call" | custom-call | tf_op jit(solution)/shard_map/second/pallas_call | solution.py:31
  25.5 9.9 %all_to_all.5.heard_ref = f32[32,1,128]{2,1,0:T(1,128)S(1)} all-to-all(f32[32,1,128]{2,1,0:T(1,128)S(1)} %get-tuple-element.28), channel_id=1, replica_groups=mesh['sens'=8,'hour'=4] {'hour','sens'}, dimensions={0} | all-to-all | bytes 32768 | tf_op jit(solution)/shard_map/all_to_all | solution.py:317
  35.4 1.3 %last.1 = (bf16[128,2048]{1,0:T(8,128)(2,1)}, f32[8,128]{1,0:T(8,128)}) custom-call(s32[1]{0:T(128)} %bitcast.me_ref.place_ref, s32[1]{0:T(128)} %bitcast.1.own_ref, f32[32,1,128]{2,1,0:T(1,128)S(1)} %all_to_all.5.heard_ref, s32[8,128]{1,0:T(8,128)S(1)} %get-tuple-element.29.zone_ref, f32[8,128]{1,0:T(8,128)S(1)} %get-tuple-element.30.area_ref, ...), custom_call_target="tpu_custom_call" | custom-call | tf_op jit(solution)/shard_map/last/pallas_call | solution.py:31
  (1 shorter events, 0.0 us)
Async XLA Ops:
  1.4 6.7 %collective-permute-start = (bf16[16,128]{1,0:T(8,128)(2,1)S(1)}, bf16[16,128]{1,0:T(8,128)(2,1)S(1)}, u32[]{:S(2)}, u32[]{:S(2)}) collective-permute-start(bf16[16,128]{1,0:T(8,128)(2,1)S(1)} %pack.1.refs_0_.one_ref), channel_id=1, source_target_pairs={{0,2},{1,3},{2,0},{3,1},{4,6},{5,7},{6,4},{7,5},{8,10},{9,11},{10,... | collective-permute-start | bytes 12296 | tf_op jit(solution)/shard_map/ppermute | solution.py:37
  8.1 4.8 %collective-permute-start.2 = (bf16[32,128]{1,0:T(8,128)(2,1)S(1)}, bf16[32,128]{1,0:T(8,128)(2,1)S(1)}, u32[]{:S(2)}, u32[]{:S(2)}) collective-permute-start(bf16[32,128]{1,0:T(8,128)(2,1)S(1)} %join.1), channel_id=1, source_target_pairs={{0,1},{1,0},{2,3},{3,2},{4,5},{5,4},{6,7},{7,6},{8,9},{9,8},{10,11... | collective-permute-start | bytes 24584 | tf_op jit(solution)/shard_map/ppermute | solution.py:37
  11.0 11.6 %collective-permute-start.1 = (s16[520,128]{1,0:T(8,128)(2,1)S(1)}, s16[520,128]{1,0:T(8,128)(2,1)S(1)}, u32[]{:S(2)}, u32[]{:S(2)}) collective-permute-start(s16[520,128]{1,0:T(8,128)(2,1)S(1)} %sun.4), channel_id=1, source_target_pairs={{0,2},{1,3},{2,0},{3,1},{4,6},{5,7},{6,4},{7,5},{8,10},{9,11},{10,... | collective-permute-start | bytes 399368 | tf_op jit(solution)/shard_map/ppermute | solution.py:37
  15.2 7.6 %collective-permute-start.3 = (s16[520,128]{1,0:T(8,128)(2,1)S(1)}, s16[520,128]{1,0:T(8,128)(2,1)S(1)}, u32[]{:S(2)}, u32[]{:S(2)}) collective-permute-start(s16[520,128]{1,0:T(8,128)(2,1)S(1)} %get-tuple-element.26), channel_id=1, source_target_pairs={{0,3},{1,2},{2,1},{3,0},{4,7},{5,6},{6,5},{7,4},{8,11},{9,10},{10,... | collective-permute-start | bytes 399368 | tf_op jit(solution)/shard_map/ppermute | solution.py:37
  17.0 8.2 %collective-permute-start.4 = (s16[520,128]{1,0:T(8,128)(2,1)S(1)}, s16[520,128]{1,0:T(8,128)(2,1)S(1)}, u32[]{:S(2)}, u32[]{:S(2)}) collective-permute-start(s16[520,128]{1,0:T(8,128)(2,1)S(1)} %get-tuple-element.27), channel_id=1, source_target_pairs={{0,1},{1,0},{2,3},{3,2},{4,5},{5,4},{6,7},{7,6},{8,9},{9,8},{10,11... | collective-permute-start | bytes 399368 | tf_op jit(solution)/shard_map/ppermute | solution.py:37

commit v6 on v4

--- a/solution.py
+++ b/solution.py
@@ -200,17 +200,23 @@
 
 def last_kernel(groups, zones, windows):
     def kernel(place_ref, own_ref, heard_ref, zone_ref, area_ref, openness_ref, closed_ref, *refs):
-        crosses, (lit_ref, step_ref) = refs[:groups], refs[groups:]
+        crosses, (lit_hbm, step_ref, lit_ref, sems) = refs[:groups], refs[groups:]
         total = jnp.sum(heard_ref[:], axis=0)
         linear, quadratic, num, den, squares = [total[:, i * zones : (i + 1) * zones] for i in range(5)]
         share = num / den
         lane = lax.broadcasted_iota(jnp.int32, share.shape, 1)
         own_share = jnp.sum(jnp.where(lane == own_ref[0], share, 0.0), keepdims=True)
         width = closed_ref.shape[1] // groups
-        for mask in range(groups):
-            at = place(place_ref, mask, width)
-            lit = closed_ref[:, at] + own_share * crosses[mask][:]
-            lit_ref[:, at] = lit.astype(jnp.bfloat16)
+        part = closed_ref.shape[0] // groups
+        copies = []
+        for r in range(groups):
+            some = pl.ds(r * part, part)
+            for mask in range(groups):
+                at = place(place_ref, mask, width)
+                lit = closed_ref[some, at] + own_share * crosses[mask][some]
+                lit_ref[some, at] = lit.astype(jnp.bfloat16)
+            copies.append(pltpu.make_async_copy(lit_ref.at[some], lit_hbm.at[some], sems.at[r]))
+            copies[r].start()
         ratio = groups * (linear + share * quadratic) / den
         rms = jnp.sqrt(jnp.sum(ratio * ratio * squares, keepdims=True) / (windows * groups) + 1e-06)
         zone = zone_ref[:]
@@ -218,6 +224,8 @@
         for z in range(zones):
             chosen = jnp.where(zone == z, ratio[:, z : z + 1], chosen)
         step_ref[:] = jnp.clip(openness_ref[:] - 0.25 * (area_ref[:] * chosen) / rms, 0.0, 1.0)
+        for c in copies:
+            c.wait()
 
     return kernel
 
@@ -235,7 +243,7 @@
     windows = area.shape[0]
     assert nbins % LANES == 0 or nbins % LANES >= 2 * kbins
     assert nbins <= 256 * LANES and width % LANES == 0 and windows % LANES == 0 and 3 * kbins <= HEAD
-    assert groups == 4 and rows % 16 == 0
+    assert groups == 4 and rows % (16 * groups) == 0
     shape = jax.ShapeDtypeStruct
     f32, bf16 = jnp.float32, jnp.bfloat16
     dma = lambda n: pltpu.SemaphoreType.DMA((n,))
@@ -320,6 +328,8 @@
         "last",
         [shape((rows, sensors), bf16), shape(tiles, f32)],
         in_specs=[SMEM] * 2 + [VMEM] * (5 + groups),
+        out_specs=[HBM, VMEM],
+        scratch_shapes=[pltpu.VMEM((rows, sensors), bf16), dma(groups)],
     )(me, own_zone, heard, zone2, area2, openness2, closed, *[crosses[mask] for mask in range(groups)])
     return (illuminance, new_openness.reshape(-1))
 

time: 36.9 us -> 37.3 us (1.011)
  Pallas kernels: 11.8 us -> 12.3 us
    pallas_call x10, Pallas kernels: 11.8 us -> 12.3 us  [call(): run(*[pltpu.with_memory_space_constraint(x, pltpu.HBM) if s is HBM else x...]
  transfers between devices with their start and end apart: 5 -> 5, of which waited for: 2 -> 2; matrix products, arithmetic and copies ran while one was open for 0% -> 0% of each run, Pallas kernels for 26% -> 25%
where the time goes in v6:
time: 37.3 us; the launch traced here: 37.1 us
  Pallas kernels  12.3 us (33%)
  blocking collectives  10.7 us (29%)
  starting transfers between devices  10.3 us (28%)
  waiting for transfers between devices  3.14 us (8%)
  between operations  0.71 us (2%)
    pallas_call x10, Pallas kernels, call(): run(*[pltpu.with_memory_space_constraint(x, pltpu.HBM) if s is HBM else x...  12.3 us
    all_to_all x1, blocking collectives, local(): heard = lax.all_to_all(sent, ('hour', 'sens'), 0, 0)  10.7 us
    ppermute x5, starting transfers between devices, exchange(): lax.ppermute(x, axis, [(i, i ^ mask) for i in range(lax.axis_size(axis))])  10.3 us
    ppermute x5, waiting for transfers between devices, exchange(): lax.ppermute(x, axis, [(i, i ^ mask) for i in range(lax.axis_size(axis))])  3.14 us
  transfers between devices with their start and end apart: 5, of which 2 were waited for; matrix products, arithmetic and copies ran while one was open for 0% of the time, Pallas kernels for 25%

profile of v6, /device:TPU:0, one launch (start us, length us, event | category | flops | bytes accessed | tf_op | source)
XLA Modules:
  0.0 37.1 jit_solution(14597880737119609240)
XLA Ops:
  0.6 0.7 %pack.1.refs_0_.one_ref = bf16[16,128]{1,0:T(8,128)(2,1)S(1)} custom-call(s32[1]{0:T(128)} %bitcast.me_ref.place_ref, s32[1]{0:T(128)} %bitcast.1.own_ref, s32[4,128]{1,0:T(4,128)} %bitcast.13, bf16[4,128]{1,0:T(4,128)(2,1)} %bitcast.14), custom_call_target="tpu_custom_call" | custom-call | tf_op jit(solution)/shard_map/pack/pallas_call | solution.py:31
  1.4 4.1 %collective-permute-start = (bf16[16,128]{1,0:T(8,128)(2,1)S(1)}, bf16[16,128]{1,0:T(8,128)(2,1)S(1)}, u32[]{:S(2)}, u32[]{:S(2)}) collective-permute-start(bf16[16,128]{1,0:T(8,128)(2,1)S(1)} %pack.1.refs_0_.one_ref), channel_id=1, source_target_pairs={{0,2},{1,3},{2,0},{3,1},{4,6},{5,7},{6,4},{7,5},{8,10},{9,11},{10,... | collective-permute-start | bytes 12296 | tf_op jit(solution)/shard_map/ppermute | solution.py:37
  5.5 2.6 %fetch.1 = (bf16[5165,512]{1,0:T(8,128)(2,1)S(1)}, f32[1,128]{1,0:T(1,128)S(1)}, s32[8,128]{1,0:T(8,128)S(1)}, f32[8,128]{1,0:T(8,128)S(1)}, f32[8,128]{1,0:T(8,128)S(1)}) custom-call(bf16[5165,512]{1,0:T(8,128)(2,1)} %coef_hbm.1, s32[8,128]{1,0:T(8,128)} %bitcast.10, f32[8,128]{1,0:T(8,128)} %bitcast.11, f32[8,128]{1,0:T(8,128)} %bitcast.12), custom_call_target="tpu_custom_call" | custom-call | tf_op jit(solution)/shard_map/fetch/pallas_call | solution.py:31
  8.1 0.0 collective-permute-done.refs_0_.two_ref
  8.1 1.6 %collective-permute-start.2 = (bf16[32,128]{1,0:T(8,128)(2,1)S(1)}, bf16[32,128]{1,0:T(8,128)(2,1)S(1)}, u32[]{:S(2)}, u32[]{:S(2)}) collective-permute-start(bf16[32,128]{1,0:T(8,128)(2,1)S(1)} %join.1), channel_id=1, source_target_pairs={{0,1},{1,0},{2,3},{3,2},{4,5},{5,4},{6,7},{7,6},{8,9},{9,8},{10,11... | collective-permute-start | bytes 24584 | tf_op jit(solution)/shard_map/ppermute | solution.py:37
  9.7 1.3 %sun.4 = s16[520,128]{1,0:T(8,128)(2,1)S(1)} custom-call(bf16[5165,512]{1,0:T(8,128)(2,1)S(1)} %get-tuple-element.20.coef_ref, bf16[16,128]{1,0:T(8,128)(2,1)S(1)} %collective-permute-done.refs_0_.two_ref), custom_call_target="tpu_custom_call" | custom-call | tf_op jit(solution)/shard_map/sun/pallas_call | solution.py:31
  11.0 1.9 %collective-permute-start.1 = (s16[520,128]{1,0:T(8,128)(2,1)S(1)}, s16[520,128]{1,0:T(8,128)(2,1)S(1)}, u32[]{:S(2)}, u32[]{:S(2)}) collective-permute-start(s16[520,128]{1,0:T(8,128)(2,1)S(1)} %sun.4), channel_id=1, source_target_pairs={{0,2},{1,3},{2,0},{3,1},{4,6},{5,7},{6,4},{7,5},{8,10},{9,11},{10,... | collective-permute-start | bytes 399368 | tf_op jit(solution)/shard_map/ppermute | solution.py:37
  12.9 0.0 collective-permute-done.2.refs_0_
  12.9 2.2 %sun.5 = (s16[520,128]{1,0:T(8,128)(2,1)S(1)}, s16[520,128]{1,0:T(8,128)(2,1)S(1)}) custom-call(bf16[5165,512]{1,0:T(8,128)(2,1)S(1)} %get-tuple-element.20.coef_ref, bf16[32,128]{1,0:T(8,128)(2,1)S(1)} %collective-permute-done.2.refs_0_), custom_call_target="tpu_custom_call" | custom-call | tf_op jit(solution)/shard_map/sun/pallas_call | solution.py:31
  15.2 0.5 %collective-permute-start.3 = (s16[520,128]{1,0:T(8,128)(2,1)S(1)}, s16[520,128]{1,0:T(8,128)(2,1)S(1)}, u32[]{:S(2)}, u32[]{:S(2)}) collective-permute-start(s16[520,128]{1,0:T(8,128)(2,1)S(1)} %get-tuple-element.26), channel_id=1, source_target_pairs={{0,1},{1,0},{2,3},{3,2},{4,5},{5,4},{6,7},{7,6},{8,9},{9,8},{10,11... | collective-permute-start | bytes 399368 | tf_op jit(solution)/shard_map/ppermute | solution.py:37
  15.7 2.1 %collective-permute-start.4 = (s16[520,128]{1,0:T(8,128)(2,1)S(1)}, s16[520,128]{1,0:T(8,128)(2,1)S(1)}, u32[]{:S(2)}, u32[]{:S(2)}) collective-permute-start(s16[520,128]{1,0:T(8,128)(2,1)S(1)} %get-tuple-element.27), channel_id=1, source_target_pairs={{0,3},{1,2},{2,1},{3,0},{4,7},{5,6},{6,5},{7,4},{8,11},{9,10},{10,... | collective-permute-start | bytes 399368 | tf_op jit(solution)/shard_map/ppermute | solution.py:37
  17.8 1.3 %sun.3.token.refs_1_ = s16[520,128]{1,0:T(8,128)(2,1)S(1)} custom-call(bf16[5165,512]{1,0:T(8,128)(2,1)S(1)} %get-tuple-element.20.coef_ref, bf16[16,128]{1,0:T(8,128)(2,1)S(1)} %pack.1.refs_0_.one_ref), custom_call_target="tpu_custom_call" | custom-call | tf_op jit(solution)/shard_map/sun/pallas_call | solution.py:31
  19.1 1.8 %base.1 = (f32[128,2048]{1,0:T(8,128)S(1)}, f32[128,2048]{1,0:T(8,128)S(1)}, bf16[128,2048]{1,0:T(8,128)(2,1)S(1)}) custom-call(s16[520,128]{1,0:T(8,128)(2,1)S(1)} %sun.3.token.refs_1_, bf16[146,128]{1,0:T(8,128)(2,1)} %bitcast.9, bf16[146,2048]{1,0:T(8,128)(2,1)} %open_hbm.1, bf16[146,2048]{1,0:T(8,128)(2,1)} %closed_hbm.1, bf16[128,2048]{1,0:T(8,128)(2,1)} %target_hbm.1), custom_call_target="tpu_custom_call" | custom-call | tf_op jit(solution)/shard_map/base/pallas_call | solution.py:31
  20.9 0.3 collective-permute-done.1.refs_0_
  21.2 0.2 first.1
  21.4 2.8 %collective-permute-done.3.refs_0_ = s16[520,128]{1,0:T(8,128)(2,1)S(1)} collective-permute-done((s16[520,128]{1,0:T(8,128)(2,1)S(1)}, s16[520,128]{1,0:T(8,128)(2,1)S(1)}, u32[]{:S(2)}, u32[]{:S(2)}) %collective-permute-start.3) | collective-permute-done | bytes 133152 | tf_op jit(solution)/shard_map/ppermute | solution.py:37
  24.3 0.0 collective-permute-done.4.refs_1_
  24.3 0.4 %second.1 = (f32[128,512]{1,0:T(8,128)S(1)}, f32[128,512]{1,0:T(8,128)S(1)}, f32[32,1,128]{2,1,0:T(1,128)S(1)}) custom-call(s32[1]{0:T(128)} %bitcast.me_ref.place_ref, s32[1]{0:T(128)} %bitcast.1.own_ref, f32[128,2048]{1,0:T(8,128)S(1)} %get-tuple-element.21.base_ref, f32[128,2048]{1,0:T(8,128)S(1)} %get-tuple-element.22.closed_ref, ...), custom_call_target="tpu_custom_call" | custom-call | tf_op jit(solution)/shard_map/second/pallas_call | solution.py:31
  24.6 10.7 %all_to_all.5.heard_ref = f32[32,1,128]{2,1,0:T(1,128)S(1)} all-to-all(f32[32,1,128]{2,1,0:T(1,128)S(1)} %get-tuple-element.28), channel_id=1, replica_groups=mesh['sens'=8,'hour'=4] {'hour','sens'}, dimensions={0} | all-to-all | bytes 32768 | tf_op jit(solution)/shard_map/all_to_all | solution.py:325
  35.4 1.7 %last.1 = (bf16[128,2048]{1,0:T(8,128)(2,1)}, f32[8,128]{1,0:T(8,128)}) custom-call(s32[1]{0:T(128)} %bitcast.me_ref.place_ref, s32[1]{0:T(128)} %bitcast.1.own_ref, f32[32,1,128]{2,1,0:T(1,128)S(1)} %all_to_all.5.heard_ref, s32[8,128]{1,0:T(8,128)S(1)} %get-tuple-element.29.zone_ref, f32[8,128]{1,0:T(8,128)S(1)} %get-tuple-element.30.area_ref, ...), custom_call_target="tpu_custom_call" | custom-call | tf_op jit(solution)/shard_map/last/pallas_call | solution.py:31
  (1 shorter events, 0.0 us)
Async XLA Ops:
  1.4 6.7 %collective-permute-start = (bf16[16,128]{1,0:T(8,128)(2,1)S(1)}, bf16[16,128]{1,0:T(8,128)(2,1)S(1)}, u32[]{:S(2)}, u32[]{:S(2)}) collective-permute-start(bf16[16,128]{1,0:T(8,128)(2,1)S(1)} %pack.1.refs_0_.one_ref), channel_id=1, source_target_pairs={{0,2},{1,3},{2,0},{3,1},{4,6},{5,7},{6,4},{7,5},{8,10},{9,11},{10,... | collective-permute-start | bytes 12296 | tf_op jit(solution)/shard_map/ppermute | solution.py:37
  8.1 4.9 %collective-permute-start.2 = (bf16[32,128]{1,0:T(8,128)(2,1)S(1)}, bf16[32,128]{1,0:T(8,128)(2,1)S(1)}, u32[]{:S(2)}, u32[]{:S(2)}) collective-permute-start(bf16[32,128]{1,0:T(8,128)(2,1)S(1)} %join.1), channel_id=1, source_target_pairs={{0,1},{1,0},{2,3},{3,2},{4,5},{5,4},{6,7},{7,6},{8,9},{9,8},{10,11... | collective-permute-start | bytes 24584 | tf_op jit(solution)/shard_map/ppermute | solution.py:37
  11.0 10.2 %collective-permute-start.1 = (s16[520,128]{1,0:T(8,128)(2,1)S(1)}, s16[520,128]{1,0:T(8,128)(2,1)S(1)}, u32[]{:S(2)}, u32[]{:S(2)}) collective-permute-start(s16[520,128]{1,0:T(8,128)(2,1)S(1)} %sun.4), channel_id=1, source_target_pairs={{0,2},{1,3},{2,0},{3,1},{4,6},{5,7},{6,4},{7,5},{8,10},{9,11},{10,... | collective-permute-start | bytes 399368 | tf_op jit(solution)/shard_map/ppermute | solution.py:37
  15.2 9.1 %collective-permute-start.3 = (s16[520,128]{1,0:T(8,128)(2,1)S(1)}, s16[520,128]{1,0:T(8,128)(2,1)S(1)}, u32[]{:S(2)}, u32[]{:S(2)}) collective-permute-start(s16[520,128]{1,0:T(8,128)(2,1)S(1)} %get-tuple-element.26), channel_id=1, source_target_pairs={{0,1},{1,0},{2,3},{3,2},{4,5},{5,4},{6,7},{7,6},{8,9},{9,8},{10,11... | collective-permute-start | bytes 399368 | tf_op jit(solution)/shard_map/ppermute | solution.py:37
  15.7 8.6 %collective-permute-start.4 = (s16[520,128]{1,0:T(8,128)(2,1)S(1)}, s16[520,128]{1,0:T(8,128)(2,1)S(1)}, u32[]{:S(2)}, u32[]{:S(2)}) collective-permute-start(s16[520,128]{1,0:T(8,128)(2,1)S(1)} %get-tuple-element.27), channel_id=1, source_target_pairs={{0,3},{1,2},{2,1},{3,0},{4,7},{5,6},{6,5},{7,4},{8,11},{9,10},{10,... | collective-permute-start | bytes 399368 | tf_op jit(solution)/shard_map/ppermute | solution.py:37
